TPU v7x, 512 devices: a whole 4x4x16 slice. The times are simulated.
512 devices in a mesh: dp: 128 (over y, z_hi, x, core), tensor: 4 (over z_lo).
Axes of the slice: x: 4, y: 4, z: 16 (z_hi: 4, z_lo: 4; z = z_hi * 4 + z_lo), core: 2. Of those that a mesh axis runs over, the one named last changes fastest.
Arguments:
- teacher_rows: bfloat16 [16384, 16384], P('dp', 'tensor'), may hold values from -24 to 24
- row_map: int32 [16384], P('dp'), may hold values from 0 to 16383, as said below
- student_hidden: bfloat16 [16384, 8192], P('dp', 'tensor'), may hold values from -6 to 6
- projected: bfloat16 [16384, 8192], P('dp', 'tensor'), may hold values from -6 to 6
- mlp_input: bfloat16 [16384, 8192], P('dp', 'tensor'), may hold values from -24 to 24
- gate_bucket: bfloat16 [8192, 512], P(None, 'tensor'), may hold values from -0.0625 to 0.0625
- up_bucket: bfloat16 [8192, 512], P(None, 'tensor'), may hold values from -0.0625 to 0.0625
- down_bucket: bfloat16 [512, 8192], P('tensor'), may hold values from -0.03125 to 0.03125
Outputs:
- grad_proj: float32 [128, 4, 4096], P(None, 'tensor', 'dp')
- grad_gate: float32 [512, 8192], P('tensor', 'dp')
- grad_up: float32 [512, 8192], P('tensor', 'dp')
Inputs may be any that keep to these rules, and one draw needn't show every extreme that they name: `row_map`: a permutation of the token ids; token id t belongs to student group t // 128; the rows of one device (aligned blocks of 128) send exactly 1 row to every student group.
All inputs are finite; a program needn't handle non-finite values.
Results may differ from a plain program's by a relative error of at most 0.0042.
Values may be sent and summed in bfloat16 or wider, within the bound.
A program may use at most 128 MiB of HBM per device.

v0:
```python
import math

import jax
import jax.numpy as jnp
from jax import lax
from jax.sharding import PartitionSpec as P

PB = 128


def contract_rows(left, right):
    return lax.dot_general(
        left, right, (((0,), (0,)), ((), ())), preferred_element_type=jnp.float32
    )


def body(
    teacher_rows, row_map, student_hidden, projected, mlp_input, gate_bucket, up_bucket, down_bucket
):
    tok_dev = row_map.shape[0]
    dp_count = lax.axis_size("dp")
    factor = 1.0 / math.sqrt(tok_dev * dp_count)
    difference = (student_hidden.astype(jnp.float32) - projected.astype(jnp.float32)) * factor
    err_local = difference.astype(jnp.bfloat16)
    err_full, inputs_full = (
        lax.all_gather(err_local, "tensor", axis=1, tiled=True),
        lax.all_gather(mlp_input, "tensor", axis=1, tiled=True),
    )
    act_grad = lax.dot_general(
        err_full, down_bucket, (((1,), (1,)), ((), ())), preferred_element_type=jnp.float32
    )
    gate_pre = jnp.dot(inputs_full, gate_bucket, preferred_element_type=jnp.float32)
    up_pre = jnp.dot(inputs_full, up_bucket, preferred_element_type=jnp.float32)
    sigmoid_gate = jax.nn.sigmoid(gate_pre)
    gate_grad = (act_grad * up_pre * sigmoid_gate * (1.0 + gate_pre * (1.0 - sigmoid_gate))).astype(
        jnp.bfloat16
    )
    up_grad = (act_grad * gate_pre * sigmoid_gate).astype(jnp.bfloat16)
    inputs_across = jnp.transpose(inputs_full)
    feature_cols = lax.all_to_all(inputs_across, "dp", split_axis=0, concat_axis=1, tiled=True)
    gate_add = lax.dot_general(
        lax.all_gather(gate_grad, "dp", axis=0, tiled=True),
        feature_cols,
        (((0,), (1,)), ((), ())),
        preferred_element_type=jnp.float32,
    )
    up_add = lax.dot_general(
        lax.all_gather(up_grad, "dp", axis=0, tiled=True),
        feature_cols,
        (((0,), (1,)), ((), ())),
        preferred_element_type=jnp.float32,
    )
    target = row_map // tok_dev
    arrangement = jnp.argsort(target, stable=True)
    sorted_rows = jnp.take(teacher_rows, arrangement, axis=0)
    sorted_slots = jnp.take(row_map % tok_dev, arrangement, axis=0)
    bucket_err = err_full[:, :PB]
    got_rows, got_slots = (
        lax.all_to_all(sorted_rows, "dp", split_axis=0, concat_axis=0, tiled=True),
        lax.all_to_all(sorted_slots, "dp", split_axis=0, concat_axis=0, tiled=True),
    )
    placed = jnp.take(got_rows, jnp.argsort(got_slots), axis=0)
    proj_term = contract_rows(bucket_err, placed)
    grad_proj = lax.psum_scatter(proj_term, "dp", scatter_dimension=1, tiled=True)
    return (grad_proj[:, None, :], gate_add, up_add)


def solution(mesh):
    in_specs = (
        P("dp", "tensor"),
        P("dp"),
        P("dp", "tensor"),
        P("dp", "tensor"),
        P("dp", "tensor"),
        P(None, "tensor"),
        P(None, "tensor"),
        P("tensor", None),
    )
    out_specs = (P(None, "tensor", "dp"), P("tensor", "dp"), P("tensor", "dp"))
    return jax.shard_map(body, mesh=mesh, in_specs=in_specs, out_specs=out_specs, check_vma=False)
```

profile of v0, /device:TPU:32, one launch (start us, length us, event | category | flops | bytes accessed | tf_op | source)
XLA Modules:
  0.0 1317.8 jit_solution(864851056988196097)
XLA Ops:
  7.2 0.0 copy-start
  7.2 0.0 all-gather.7.cloned.1.call-start
  7.2 2.2 copy.19
  9.4 0.0 all-gather.7.cloned.1.call-update
  9.4 0.0 all-gather.5.cloned.1.call-start
  9.5 2.2 multiply_convert_fusion
  11.6 0.0 all-gather.5.cloned.1.call-update
  11.7 0.0 all-gather.9.cloned.1.call-start
  11.7 57.0 %all-gather.7.cloned.1.call-done = bf16[128,8192]{0,1:T(8,128)(2,1)} async-done(((bf16[128,2048]{0,1:T(8,128)(2,1)}), bf16[128,8192]{0,1:T(8,128)(2,1)}) %all-gather.7.cloned.1.call-update) | async-done | bytes 2097168 | tf_op jit(solution)/shard_map/all_gather | solution.py:27
  68.8 3.0 fusion.15
  71.7 54.1 %all-gather.5.cloned.1.call-done = bf16[128,8192]{1,0:T(8,128)(2,1)} async-done(((bf16[128,2048]{1,0:T(8,128)(2,1)}), bf16[128,8192]{1,0:T(8,128)(2,1)}) %all-gather.5.cloned.1.call-update) | async-done | bytes 2097168 | tf_op jit(solution)/shard_map/all_gather | solution.py:26
  125.8 0.0 copy-done
  125.8 0.0 copy-start.2
  125.8 0.0 copy-start.3
  125.8 3.1 multiply_convert_fusion.1
  128.9 0.0 copy-done.2
  128.9 0.0 copy-done.3
  128.9 0.0 copy-start.4
  128.9 0.0 copy-start.1
  128.9 1.4 fusion.8
  130.3 0.0 all-gather.9.cloned.1.call-update
  130.3 0.0 copy-done.4
  130.4 2.5 sort.34
  132.9 1.2 gather_fusion
  134.2 0.7 copy.17
  134.9 17.3 %all-to-all-start.1 = ((s32[128,1,1]{2,1,0:T(1,128)}), s32[128,1,1]{2,1,0:T(1,128)S(1)}, u32[]{:S(2)}, u32[]{:S(2)}) async-start(s32[128,1,1]{2,1,0:T(1,128)} %copy.17), calls=%async_computation.1 | async-start | bytes 131072 | tf_op jit(solution)/shard_map/all_to_all | solution.py:60
  152.2 0.0 copy-done.1
  152.2 2.2 gather_fusion.1
  154.4 1.4 select_bitcast_fusion
  155.8 0.5 broadcast.57
  156.3 2.1 reduce.1
  158.4 2.7 reshape.58
  161.0 8.3 all-to-all-done.1
  169.3 10.3 all-to-all-start
  179.6 0.0 all-gather.11.cloned.1.call-start
  179.7 0.5 all-gather.11.cloned.1.call-update
  180.2 59.0 %all-to-all-done = bf16[128,2,2048]{2,1,0:T(2,128)(2,1)S(1)} async-done(((bf16[128,2,2048]{2,1,0:T(2,128)(2,1)}), bf16[128,2,2048]{2,1,0:T(2,128)(2,1)S(1)}, u32[]{:S(2)}, u32[]{:S(2)}) %all-to-all-start) | async-done | bytes 1048608 | tf_op jit(solution)/shard_map/all_to_all | solution.py:59
  239.2 11.6 all-to-all-start.2
  250.8 0.2 reduce-scatter.2.cloned.1.call-start
  251.0 2.4 reduce
  253.4 2.5 sort.35
  256.0 3.5 reshape.59
  259.5 2.7 copy.32
  262.2 2.2 gather_fusion.2
  264.4 3.2 fusion.9
  267.5 0.0 reduce-scatter.2.cloned.1.call-update
  267.6 80.4 %all-gather.9.cloned.1.call-done = bf16[16384,128]{1,0:T(8,128)(2,1)} async-done(((bf16[128,128]{1,0:T(8,128)(2,1)}), bf16[16384,128]{1,0:T(8,128)(2,1)}) %all-gather.9.cloned.1.call-update) | async-done | bytes 4194320 | tf_op jit(solution)/shard_map/all_gather | solution.py:42
  347.9 15.2 %all-to-all-done.2 = bf16[128,64,128]{2,1,0:T(8,128)(2,1)} async-done(((bf16[128,64,128]{2,1,0:T(8,128)(2,1)}), bf16[128,64,128]{2,1,0:T(8,128)(2,1)}, u32[]{:S(2)}, u32[]{:S(2)}) %all-to-all-start.2) | async-done | bytes 2097184 | tf_op jit(solution)/shard_map/all_to_all | solution.py:40
  363.1 4.4 fusion
  367.5 121.4 %all-gather.11.cloned.1.call-done = bf16[16384,128]{1,0:T(8,128)(2,1)} async-done(((bf16[128,128]{1,0:T(8,128)(2,1)}), bf16[16384,128]{1,0:T(8,128)(2,1)}) %all-gather.11.cloned.1.call-update) | async-done | bytes 4194320 | tf_op jit(solution)/shard_map/all_gather | solution.py:48
  488.9 4.4 fusion.2
  493.3 818.0 %reduce-scatter.2.cloned.1.call-done = f32[128,32]{0,1:T(8,128)} async-done(((f32[128,4096]{0,1:T(8,128)}), f32[128,32]{0,1:T(8,128)}) %reduce-scatter.2.cloned.1.call-update) | async-done | bytes 16400 | tf_op jit(solution)/shard_map/reduce_scatter | solution.py:64
  (9 shorter events, 0.1 us)
Async XLA Ops:
  7.2 118.7 %copy-start = (bf16[128,8192]{1,0:T(8,128)(2,1)S(1)}, bf16[128,8192]{1,0:T(8,128)(2,1)}, u32[]{:S(2)}) copy-start(bf16[128,8192]{1,0:T(8,128)(2,1)} %param.17) | copy-start | bytes 6291460
  7.2 61.6 %all-gather.7.cloned.1.call-start = ((), (), s32[]{:S(2)}) async-start(), calls=%async_computation.6 | async-start | bytes 2621440 | tf_op jit(solution)/shard_map/all_gather | solution.py:27
  9.4 116.4 %all-gather.5.cloned.1.call-start = ((), (), s32[]{:S(2)}) async-start(), calls=%async_computation.4 | async-start | bytes 2621440 | tf_op jit(solution)/shard_map/all_gather | solution.py:26
  11.7 336.3 %all-gather.9.cloned.1.call-start = ((), (), s32[]{:S(2)}) async-start(), calls=%async_computation.7 | async-start | bytes 4227072 | tf_op jit(solution)/shard_map/all_gather | solution.py:42
  125.8 3.1 copy-start.2
  125.8 3.1 copy-start.3
  128.9 1.4 copy-start.4
  128.9 23.3 %copy-start.1 = (bf16[128,4096]{1,0:T(8,128)(2,1)S(1)}, bf16[128,4096]{1,0:T(8,128)(2,1)}, u32[]{:S(2)}) copy-start(bf16[128,4096]{1,0:T(8,128)(2,1)} %param.10) | copy-start | bytes 3145732
  134.9 34.4 %all-to-all-start.1 = ((s32[128,1,1]{2,1,0:T(1,128)}), s32[128,1,1]{2,1,0:T(1,128)S(1)}, u32[]{:S(2)}, u32[]{:S(2)}) async-start(s32[128,1,1]{2,1,0:T(1,128)} %copy.17), calls=%async_computation.1 | async-start | bytes 131072 | tf_op jit(solution)/shard_map/all_to_all | solution.py:60
  169.3 69.8 %all-to-all-start = ((bf16[128,2,2048]{2,1,0:T(2,128)(2,1)}), bf16[128,2,2048]{2,1,0:T(2,128)(2,1)S(1)}, u32[]{:S(2)}, u32[]{:S(2)}) async-start(bf16[128,2,2048]{2,1,0:T(2,128)(2,1)} %reshape.58), calls=%async_computation | async-start | bytes 2097152 | tf_op jit(solution)/shard_map/all_to_all | solution.py:59
  179.6 309.2 %all-gather.11.cloned.1.call-start = ((), (), s32[]{:S(2)}) async-start(), calls=%async_computation.8 | async-start | bytes 4227072 | tf_op jit(solution)/shard_map/all_gather | solution.py:48
  239.2 123.9 %all-to-all-start.2 = ((bf16[128,64,128]{2,1,0:T(8,128)(2,1)}), bf16[128,64,128]{2,1,0:T(8,128)(2,1)}, u32[]{:S(2)}, u32[]{:S(2)}) async-start(bf16[128,64,128]{2,1,0:T(8,128)(2,1)} %bitcast.33), calls=%async_computation.3 | async-start | bytes 4194304 | tf_op jit(solution)/shard_map/all_to_all | solution.py:40
  250.8 1060.5 %reduce-scatter.2.cloned.1.call-start = ((), (), s32[]{:S(2)}) async-start(), calls=%async_computation.5 | async-start | bytes 2113536 | tf_op jit(solution)/shard_map/reduce_scatter | solution.py:64
Sparse Core Ops, SparseCore 0:
  10.1 58.5 all-gather.6
  70.8 54.9 all-gather.4
  130.9 217.0 all-gather.8
  352.8 136.0 all-gather.10
  492.1 819.1 reduce-scatter.1
where the time goes:
time: 1320 us
  waiting for transfers between devices  1210 us (92%)
  starting transfers between devices  39.6 us (3%)
  matrix products  19.3 us (1%)
  local copies, waits for them, and re-layouts  17.9 us (1%)
  between operations  13.9 us (1%)
    reduce_scatter x1, waiting for transfers between devices, body(): lax.psum_scatter(proj_term, 'dp', scatter_dimension=1, tiled=True)  818 us
    all_gather x1, waiting for transfers between devices, body(): lax.all_gather(up_grad, 'dp', axis=0, tiled=True)  121 us
    all_gather x1, waiting for transfers between devices, body(): lax.all_gather(gate_grad, 'dp', axis=0, tiled=True)  80.4 us
    all_to_all x1, waiting for transfers between devices, body(): lax.all_to_all(sorted_rows, 'dp', split_axis=0, concat_axis=0, tiled=True)  59 us
    all_gather x1, waiting for transfers between devices, body(): lax.all_gather(mlp_input, 'tensor', axis=1, tiled=True)  57 us
    all_gather x1, waiting for transfers between devices, body(): lax.all_gather(err_local, 'tensor', axis=1, tiled=True)  54.1 us
  transfers between devices with their start and end apart: 8, of which 8 were waited for; matrix products, arithmetic and copies ran while one was open for 3% of the time, Pallas kernels for 0%

commit v1 on v0

v1 whole, which is shorter than its diff:
```python
import functools

import jax
import jax.numpy as jnp
from jax import lax
from jax.experimental import pallas as pl
from jax.experimental.pallas import tpu as pltpu
from jax.sharding import PartitionSpec as P

MESH = pl.DeviceIdType.MESH
BF = jnp.bfloat16
F32 = jnp.float32
NC = 2
HALVES = 2


def sizes(mesh, pb):
    nt = mesh.shape["tensor"]
    rest = mesh.shape["dp"] // (nt * NC)
    nx = 4 if rest == 16 else 2
    return dict(NY=nt, NZ=rest // nx, NX=nx, NT=nt, PB=pb)


def kernel(
    dims, teacher, rowmap, student, projected, mlp, gate, up, down, out,
    Xs, stu, prj, err, wgu, WdS, tea, TT, TA, XA, XT, G, E, pre, actp, actr, eb,
    RM, S0, S1, S2, S3, S4, msg, RB,
    ld, z_s, z_r, wd_s, wd_r, eb_s, eb_r, rm_s, rm_r, ea_s, ea_r, ea_l, xa_s, xa_r, ta_s, ta_r,
    act_s, act_r, e_s, e_r, g_s, g_r, rb_s, rb_r,
):
    NY, NZ, NX, NT, PB = (dims[k] for k in ("NY", "NZ", "NX", "NT", "PB"))
    NJ = NZ // NC
    TOK, S = mlp.shape
    H = gate.shape[1]
    DP = NY * NZ * NX * NC
    DTs = teacher.shape[1]
    L = S // (NZ * NX)
    LT = DTs // (NY * NZ * NX)
    NB = NY * NC * NX
    d = lax.axis_index("dp")
    t = lax.axis_index("tensor")
    c = lax.rem(d, NC)
    x = lax.rem(lax.div(d, NC), NX)
    zh = lax.rem(lax.div(d, NC * NX), NZ)
    y = lax.div(d, NC * NX * NZ)
    b = (y * NC + c) * NX + x
    factor = float(TOK * DP) ** -0.5
    drains = []

    def did(y_, zh_, x_, c_, t_):
        return (((y_ * NZ + zh_) * NX + x_) * NC + c_, t_)

    def send(src, dst, ssem, rsem, where):
        copy = pltpu.make_async_remote_copy(
            src_ref=src, dst_ref=dst, send_sem=ssem, recv_sem=rsem, device_id=where, device_id_type=MESH
        )
        copy.start()
        drains.append((None, copy))

    def send_if(cond, src, dst, ssem, rsem, where):
        @pl.when(cond)
        def _():
            pltpu.make_async_remote_copy(
                src_ref=src(), dst_ref=dst(), send_sem=ssem, recv_sem=rsem, device_id=where, device_id_type=MESH
            ).start()

    def arrived(ref, sem):
        pltpu.make_async_copy(ref, ref, sem).wait()

    def al(v, m):
        return pl.multiple_of(v, m)

    half = TOK // HALVES

    def rows_of(h):
        return pl.ds(h * half, half)

    loads = [
        pltpu.make_async_copy(rowmap, RM.at[y, zh, x, c], ld.at[0]),
        pltpu.make_async_copy(student, stu, ld.at[1]),
        pltpu.make_async_copy(projected, prj, ld.at[2]),
        pltpu.make_async_copy(mlp, Xs.at[t], ld.at[3]),
        pltpu.make_async_copy(teacher, tea, ld.at[4]),
        pltpu.make_async_copy(gate, wgu.at[:, pl.ds(0, H)], ld.at[5]),
        pltpu.make_async_copy(up, wgu.at[:, pl.ds(H, H)], ld.at[6]),
        pltpu.make_async_copy(down.at[:, pl.ds(al(t * S, S), S)], WdS.at[t], ld.at[7]),
    ]
    for copy in loads:
        copy.start()

    barrier = pltpu.get_barrier_semaphore()

    def greet(q, carry):
        q_x = lax.rem(q, NX)
        q_c = lax.rem(lax.div(q, NX), NC)
        q_y = lax.div(q, NX * NC)

        @pl.when(q != b)
        def _():
            pl.semaphore_signal(barrier, inc=1, device_id=did(q_y, zh, q_x, q_c, t), device_id_type=MESH)

        return carry

    lax.fori_loop(0, NB, greet, 0)
    for o in range(1, NZ):
        for q_c in range(NC):
            pl.semaphore_signal(
                barrier, inc=1, device_id=did(y, lax.rem(zh + o, NZ), x, q_c, t), device_id_type=MESH
            )
    for o in range(1, NT):
        pl.semaphore_signal(barrier, inc=1, device_id=(d, lax.rem(t + o, NT)), device_id_type=MESH)
    pl.semaphore_wait(barrier, NB - 1 + (NZ - 1) * NC + NT - 1)

    def z_send(k, h):
        sr, sl = t - k, t + k
        rows = rows_of(h)
        src_r = (lambda: mlp.at[rows]) if k == 0 else (lambda: Xs.at[sr, rows])
        src_l = (lambda: mlp.at[rows]) if k == 0 else (lambda: Xs.at[sl, rows])
        send_if((sr >= 0) & (t < NT - 1), src_r, lambda: Xs.at[sr, rows], z_s.at[0, k, h], z_r.at[0, k, h], (d, t + 1))
        send_if((sl <= NT - 1) & (t > 0), src_l, lambda: Xs.at[sl, rows], z_s.at[1, k, h], z_r.at[1, k, h], (d, t - 1))

    def z_drain(k, h):
        sr, sl = t - k, t + k

        @pl.when((sr >= 0) & (t < NT - 1))
        def _():
            arrived(Xs.at[sr, rows_of(h)], z_s.at[0, k, h])

        @pl.when((sl <= NT - 1) & (t > 0))
        def _():
            arrived(Xs.at[sl, rows_of(h)], z_s.at[1, k, h])

    def z_wait(k, h):
        @pl.when(t - k - 1 >= 0)
        def _():
            arrived(Xs.at[t - k - 1, rows_of(h)], z_r.at[0, k, h])

        @pl.when(t + k + 1 <= NT - 1)
        def _():
            arrived(Xs.at[t + k + 1, rows_of(h)], z_r.at[1, k, h])

    def a2a(s):
        def one(q, carry):
            q_x, q_c = lax.div(q, NC), lax.rem(q, NC)
            own = (s == y) & (q_x == x) & (q_c == c)
            for j in range(NJ):
                src = Xs.at[s, :, pl.ds(al(((q_c * NJ + j) * NX + q_x) * L, L), L)]
                dst = XA.at[pl.ds(al(b * TOK, TOK), TOK), pl.ds(j * L, L)]

                @pl.when(own)
                def _():
                    pltpu.make_async_copy(src, dst, xa_r).start()

                @pl.when(jnp.logical_not(own))
                def _():
                    pltpu.make_async_remote_copy(
                        src_ref=src, dst_ref=dst, send_sem=xa_s, recv_sem=xa_r,
                        device_id=did(s, zh, q_x, q_c, t), device_id_type=MESH,
                    ).start()

            return carry

        lax.fori_loop(0, NX * NC, one, 0)

    def add_pre(s):
        pre[...] += jnp.dot(Xs[s], wgu[pl.ds(al(s * S, S), S), :], preferred_element_type=F32)

    def consume(k):
        @pl.when(t - k - 1 >= 0)
        def _():
            a2a(t - k - 1)

        @pl.when(t + k + 1 <= NT - 1)
        def _():
            a2a(t + k + 1)

        @pl.when(t - k - 1 >= 0)
        def _():
            add_pre(t - k - 1)

        @pl.when(t + k + 1 <= NT - 1)
        def _():
            add_pre(t + k + 1)

    for h in range(HALVES):
        z_send(0, h)

    HR = H // (NX * NC)
    wrow = pl.ds(al((c * NX + x) * HR, HR), HR)
    for o in range(1, NT):
        p = lax.rem(t + o, NT)
        send(down.at[wrow, pl.ds(al(p * S, S), S)], WdS.at[t, wrow], wd_s.at[0, o - 1], wd_r.at[0, o - 1], (d, p))

    loads[0].wait()
    send(RM.at[y, zh, x, c], RM.at[y, zh, x, c], rm_s.at[0], rm_r.at[0, 0], did(y, zh, x, 1 - c, t))

    loads[1].wait()
    loads[2].wait()

    def err_rows(i, carry):
        r = pl.ds(al(i * 16, 16), 16)
        err[r, :] = ((stu[r, :].astype(F32) - prj[r, :].astype(F32)) * factor).astype(BF)
        return carry

    lax.fori_loop(0, TOK // 16, err_rows, 0)

    @pl.when(t == 0)
    def _():
        eb[...] = err[:, 0:PB]

    for o in range(1, NT):
        send_if(t == 0, lambda: eb, lambda: eb, eb_s.at[o - 1], eb_r, (d, o))

    loads[3].wait()
    a2a(t)

    arrived(RM.at[y, zh, x, 1 - c], rm_r.at[0, 0])
    for o in range(1, NX):
        q = lax.rem(x + o, NX)
        send(RM.at[y, zh, x], RM.at[y, zh, x], rm_s.at[1], rm_r.at[1, o - 1], did(y, zh, q, c, t))

    loads[4].wait()
    TC = DTs // 8

    def flip(i, carry):
        TT[pl.ds(al(i * TC, TC), TC), :] = jnp.transpose(tea[:, pl.ds(al(i * TC, TC), TC)])
        return carry

    lax.fori_loop(0, 4, flip, 0)

    for o in range(1, NX):
        arrived(RM.at[y, zh, lax.rem(x + NX - o, NX)], rm_r.at[1, o - 1])
    for o in range(1, NY):
        send(RM.at[y, zh], RM.at[y, zh], rm_s.at[2], rm_r.at[2, o - 1], did(lax.rem(y + o, NY), zh, x, c, t))

    for o in range(1, NT):
        p = lax.rem(t + NT - o, NT)
        arrived(WdS.at[p, wrow], wd_r.at[0, o - 1])
    for o in range(1, NT):
        p = lax.rem(t + NT - o, NT)
        for u in range(1, NX):
            send(
                WdS.at[p, wrow], WdS.at[p, wrow], wd_s.at[1, o - 1], wd_r.at[1, (o - 1) * (NX - 1) + u - 1],
                did(y, zh, lax.rem(x + u, NX), c, t),
            )

    lax.fori_loop(4, 8, flip, 0)

    for o in range(1, NY):
        arrived(RM.at[lax.rem(y + NY - o, NY), zh], rm_r.at[2, o - 1])
    for o in range(1, NZ):
        send(RM.at[:, zh], RM.at[:, zh], rm_s.at[3], rm_r.at[3, o - 1], did(y, lax.rem(zh + o, NZ), x, c, t))

    loads[5].wait()
    loads[6].wait()
    loads[7].wait()
    pre[...] = jnp.dot(Xs[t], wgu[pl.ds(al(t * S, S), S), :], preferred_element_type=F32)

    for o in range(1, NZ):
        arrived(RM.at[:, lax.rem(zh + NZ - o, NZ)], rm_r.at[3, o - 1])

    @pl.when(t != 0)
    def _():
        arrived(eb, eb_r)

    ids = RM[...].reshape(DP, TOK)
    slot = jnp.sum(jnp.where(lax.div(ids, TOK) == d, lax.rem(ids, TOK), 0), axis=1, keepdims=True)
    pick = (lax.broadcasted_iota(jnp.int32, (DP, TOK), 1) == slot).astype(F32).astype(BF)
    S0[...] = jnp.dot(pick, eb[...], preferred_element_type=F32).reshape(S0.shape)
    keep = [pltpu.make_async_copy(S0.at[y], S1.at[y], ea_l.at[0])]
    keep[0].start()
    for o in range(1, NY):
        q = lax.rem(y + o, NY)
        send(S0.at[q], S1.at[y], ea_s.at[0], ea_r.at[0, o - 1], did(q, zh, x, c, t))

    def z_step(k):
        for h in range(HALVES):
            z_wait(k, h)
            if k + 1 < NT - 1:
                z_send(k + 1, h)
        consume(k)

    if NT > 1:
        z_step(0)

    for o in range(1, NT):
        p = lax.rem(t + NT - o, NT)
        for u in range(1, NX):
            r = pl.ds(al((c * NX + lax.rem(x + NX - u, NX)) * HR, HR), HR)
            arrived(WdS.at[p, r], wd_r.at[1, (o - 1) * (NX - 1) + u - 1])
    crow = pl.ds(al(c * NX * HR, NX * HR), NX * HR)
    orow = pl.ds(al((1 - c) * NX * HR, NX * HR), NX * HR)
    for o in range(1, NT):
        p = lax.rem(t + NT - o, NT)
        send(WdS.at[p, crow], WdS.at[p, crow], wd_s.at[2, o - 1], wd_r.at[2, o - 1], did(y, zh, x, 1 - c, t))

    keep[0].wait()
    for o in range(1, NY):
        arrived(S1.at[lax.rem(y + NY - o, NY)], ea_r.at[0, o - 1])
    keep.append(pltpu.make_async_copy(S1.at[:, zh], S2.at[:, zh], ea_l.at[1]))
    keep[1].start()
    for o in range(1, NZ):
        q = lax.rem(zh + o, NZ)
        send(S1.at[:, q], S2.at[:, zh], ea_s.at[1], ea_r.at[1, o - 1], did(y, q, x, c, t))

    def tea_out(q, carry):
        q_x = lax.rem(q, NX)
        q_c = lax.rem(lax.div(q, NX), NC)
        q_y = lax.div(q, NX * NC)
        for j in range(NJ):
            src = TT.at[pl.ds(al(((q_y * NZ + q_c * NJ + j) * NX + q_x) * LT, LT), LT), :]
            dst = TA.at[pl.ds(j * LT, LT), pl.ds(al(b * TOK, TOK), TOK)]

            @pl.when(q == b)
            def _():
                pltpu.make_async_copy(src, dst, ta_r).start()

            @pl.when(q != b)
            def _():
                pltpu.make_async_remote_copy(
                    src_ref=src, dst_ref=dst, send_sem=ta_s, recv_sem=ta_r,
                    device_id=did(q_y, zh, q_x, q_c, t), device_id_type=MESH,
                ).start()

        return carry

    lax.fori_loop(0, NB, tea_out, 0)

    for o in range(1, NT):
        p = lax.rem(t + NT - o, NT)
        arrived(WdS.at[p, orow], wd_r.at[2, o - 1])
    for p in range(NT):
        actp[p] = lax.dot_general(err[...], WdS[p], (((1,), (1,)), ((), ())), preferred_element_type=F32)
    for o in range(1, NT):
        p = lax.rem(t + o, NT)
        send(actp.at[p], actr.at[o - 1], act_s.at[o - 1], act_r.at[o - 1], (d, p))

    keep[1].wait()
    for o in range(1, NZ):
        arrived(S2.at[:, lax.rem(zh + NZ - o, NZ)], ea_r.at[1, o - 1])
    keep.append(pltpu.make_async_copy(S2.at[:, :, x], S3.at[:, :, x], ea_l.at[2]))
    keep[2].start()
    for o in range(1, NX):
        q = lax.rem(x + o, NX)
        send(S2.at[:, :, q], S3.at[:, :, x], ea_s.at[2], ea_r.at[2, o - 1], did(y, zh, q, c, t))

    if NT > 2:
        z_step(1)

    keep[2].wait()
    for o in range(1, NX):
        arrived(S3.at[:, :, lax.rem(x + NX - o, NX)], ea_r.at[2, o - 1])
    keep.append(pltpu.make_async_copy(S3.at[:, :, :, c], S4.at[:, :, :, c], ea_l.at[3]))
    keep[3].start()
    send(S3.at[:, :, :, 1 - c], S4.at[:, :, :, c], ea_s.at[3], ea_r.at[3, 0], did(y, zh, x, 1 - c, t))
    keep[3].wait()
    arrived(S4.at[:, :, :, 1 - c], ea_r.at[3, 0])

    brow = pl.ds(al(b * TOK, TOK), TOK)

    def block(q_y, q_c, q_x):
        return pl.ds(al(((q_y * NC + q_c) * NX + q_x) * TOK, TOK), TOK)

    def group(q_y, q_c):
        return pl.ds(al((q_y * NC + q_c) * NX * TOK, NX * TOK), NX * TOK)

    mine = RM[y, zh, x, c]
    order = (lax.broadcasted_iota(jnp.int32, (DP, TOK), 0) == lax.div(mine, TOK)).astype(F32).astype(BF)
    E[brow, :] = lax.dot_general(
        order, S4[...].reshape(DP, PB).astype(BF), (((0,), (0,)), ((), ())), preferred_element_type=F32
    ).astype(BF)
    for o in range(1, NX):
        send(E.at[brow], E.at[brow], e_s.at[0], e_r.at[0, o - 1], did(y, zh, lax.rem(x + o, NX), c, t))
    for o in range(1, NX):
        arrived(E.at[block(y, c, lax.rem(x + NX - o, NX))], e_r.at[0, o - 1])
    for o in range(1, NY):
        send(E.at[group(y, c)], E.at[group(y, c)], e_s.at[1], e_r.at[1, o - 1], did(lax.rem(y + o, NY), zh, x, c, t))

    if NT > 3:
        z_step(2)

    for o in range(1, NY):
        arrived(E.at[group(lax.rem(y + NY - o, NY), c)], e_r.at[1, o - 1])
    for q_y in range(NY):
        send(E.at[group(q_y, c)], E.at[group(q_y, c)], e_s.at[2], e_r.at[2, q_y], did(y, zh, x, 1 - c, t))

    act = actp[t]
    for o in range(1, NT):
        arrived(actr.at[o - 1], act_r.at[o - 1])
        act = act + actr[o - 1]
    gate_pre, up_pre = pre[:, 0:H], pre[:, H : 2 * H]
    sig = jax.nn.sigmoid(gate_pre)
    G[brow, 0:H] = (act * up_pre * sig * (1.0 + gate_pre * (1.0 - sig))).astype(BF)
    G[brow, H : 2 * H] = (act * gate_pre * sig).astype(BF)
    lo, hi = pl.ds(0, H), pl.ds(H, H)
    for o in range(1, NX):
        send(G.at[brow, lo], G.at[brow, lo], g_s.at[0], g_r.at[0, o - 1], did(y, zh, lax.rem(x + o, NX), c, t))
    for o in range(1, NY):
        send(G.at[brow, hi], G.at[brow, hi], g_s.at[1], g_r.at[1, o - 1], did(lax.rem(y + o, NY), zh, x, c, t))
    for o in range(1, NX):
        arrived(G.at[block(y, c, lax.rem(x + NX - o, NX)), lo], g_r.at[0, o - 1])
    for o in range(1, NY):
        send(
            G.at[group(y, c), lo], G.at[group(y, c), lo], g_s.at[2], g_r.at[2, o - 1],
            did(lax.rem(y + o, NY), zh, x, c, t),
        )
    for o in range(1, NY):
        arrived(G.at[block(lax.rem(y + NY - o, NY), c, x), hi], g_r.at[1, o - 1])
    for o in range(1, NX):
        for q_y in range(NY):
            send(
                G.at[block(q_y, c, x), hi], G.at[block(q_y, c, x), hi], g_s.at[3],
                g_r.at[3, (o - 1) * NY + q_y], did(y, zh, lax.rem(x + o, NX), c, t),
            )

    arrived(XA, xa_r)
    CH = NB * TOK // 8

    def flip_x(i, carry):
        XT[:, pl.ds(al(i * CH, CH), CH)] = jnp.transpose(XA[pl.ds(al(i * CH, CH), CH), :])
        return carry

    lax.fori_loop(0, 8, flip_x, 0)

    for o in range(1, NY):
        arrived(G.at[group(lax.rem(y + NY - o, NY), c), lo], g_r.at[2, o - 1])
    for o in range(1, NX):
        for q_y in range(NY):
            arrived(G.at[block(q_y, c, lax.rem(x + NX - o, NX)), hi], g_r.at[3, (o - 1) * NY + q_y])
    for q_y in range(NY):
        send(G.at[group(q_y, c)], G.at[group(q_y, c)], g_s.at[4], g_r.at[4, q_y], did(y, zh, x, 1 - c, t))

    for q_y in range(NY):
        arrived(E.at[group(q_y, 1 - c)], e_r.at[2, q_y])
    arrived(TA, ta_r)
    proj = jnp.dot(TA[...], E[...], preferred_element_type=F32)
    KG = NX * TOK

    def part(q_y, q_c):
        at = al((q_y * NC + q_c) * KG, KG)
        return jnp.dot(XT[:, pl.ds(at, KG)], G[pl.ds(at, KG), :], preferred_element_type=F32)

    total = part(0, c)
    for q_y in range(1, NY):
        total = total + part(q_y, c)
    for q_y in range(NY):
        arrived(G.at[group(q_y, 1 - c)], g_r.at[4, q_y])
        total = total + part(q_y, 1 - c)

    R, RP = L // NC, LT // NC
    for j in range(NJ):
        for q_c in range(NC):
            at = j * L + q_c * R
            msg[j, q_c, 0:R, :] = total[at : at + R, 0:H].astype(BF)
            msg[j, q_c, R : 2 * R, :] = total[at : at + R, H : 2 * H].astype(BF)
            at = j * LT + q_c * RP
            msg[j, q_c, 2 * R : 2 * R + RP, :] = proj[at : at + RP, :].astype(BF)
    for j in range(NJ):
        q_z = c * NJ + j
        for q_c in range(NC):
            own = (q_z == zh) & (c == q_c)

            @pl.when(own)
            def _():
                pltpu.make_async_copy(msg.at[j, q_c], RB.at[zh], rb_r.at[zh]).start()

            send_if(
                jnp.logical_not(own), lambda: msg.at[j, q_c], lambda: RB.at[zh], rb_s.at[j, q_c], rb_r.at[zh],
                did(y, q_z, x, q_c, t),
            )
    for q in range(NZ):
        arrived(RB.at[q], rb_r.at[q])
    result = RB[0].astype(F32)
    for q in range(1, NZ):
        result = result + RB[q].astype(F32)
    out[...] = result

    for _, copy in drains:
        copy.wait_send()
    for k in range(NT - 1):
        for h in range(HALVES):
            z_drain(k, h)
    for o in range(1, NT):
        @pl.when(t == 0)
        def _():
            arrived(eb, eb_s.at[o - 1])
    for j in range(NJ):
        for q_c in range(NC):
            @pl.when(jnp.logical_not((c * NJ + j == zh) & (c == q_c)))
            def _():
                arrived(msg.at[j, q_c], rb_s.at[j, q_c])

    def drain_a2a(q, carry):
        for j in range(NJ):
            arrived(XA.at[pl.ds(0, TOK), pl.ds(j * L, L)], xa_s)
            arrived(TA.at[pl.ds(j * LT, LT), pl.ds(0, TOK)], ta_s)
        return carry

    lax.fori_loop(0, NB - 1, drain_a2a, 0)


def solution(mesh, pb=128):
    dims = sizes(mesh, pb)
    NY, NZ, NX, NT = (dims[k] for k in ("NY", "NZ", "NX", "NT"))

    def body(teacher_rows, row_map, student_hidden, projected, mlp_input, gate_bucket, up_bucket, down_bucket):
        TOK, S = mlp_input.shape
        F, H = gate_bucket.shape
        DTs = teacher_rows.shape[1]
        NJ = NZ // NC
        L, LT = S // (NZ * NX), DTs // (NY * NZ * NX)
        NB = NY * NC * NX
        R, RP = L // NC, LT // NC
        V, D = pltpu.VMEM, pltpu.SemaphoreType.DMA
        rows5 = (NY, NZ, NX, NC, 1, TOK)
        scratch = [
            V((NT, TOK, S), BF), V((TOK, S), BF), V((TOK, S), BF), V((TOK, S), BF),
            V((F, 2 * H), BF), V((NT, H, S), BF),
            V((TOK, DTs), BF), V((DTs, TOK), BF), V((NJ * LT, NB * TOK), BF),
            V((NB * TOK, NJ * L), BF), V((NJ * L, NB * TOK), BF),
            V((NB * TOK, 2 * H), BF), V((NB * TOK, pb), BF),
            V((TOK, 2 * H), F32), V((NT, TOK, H), F32), V((NT - 1, TOK, H), F32), V((TOK, pb), BF),
            V(rows5, jnp.int32),
        ]
        scratch += [V((NY, NZ, NX, NC, 1, pb), F32)] * 5
        scratch += [V((NJ, NC, 2 * R + RP, H), BF), V((NZ, 2 * R + RP, H), BF)]
        K = NT - 1
        scratch += [
            D((8,)), D((2, K, HALVES)), D((2, K, HALVES)),
            D((3, K)), D((3, K * max(NX - 1, 1))),
            D((K,)), D,
            D((4,)), D((4, 3)), D((4,)), D((4, 3)), D((4,)),
            D, D, D, D,
            D((K,)), D((K,)),
            D((3,)), D((3, 4)), D((5,)), D((5, 12)),
            D((NJ, NC)), D((NZ,)),
        ]
        res = pl.pallas_call(
            functools.partial(kernel, dims),
            out_shape=jax.ShapeDtypeStruct((2 * R + RP, H), F32),
            in_specs=[pl.BlockSpec(memory_space=pl.ANY)] * 8,
            out_specs=pl.BlockSpec(memory_space=pltpu.VMEM),
            scratch_shapes=scratch,
            compiler_params=pltpu.CompilerParams(
                collective_id=0, has_side_effects=True, vmem_limit_bytes=48 * 1024 * 1024
            ),
        )(teacher_rows, row_map.reshape(1, TOK), student_hidden, projected, mlp_input, gate_bucket, up_bucket, down_bucket)
        return res[2 * R :].T[:, None, :], res[:R].T, res[R : 2 * R].T

    in_specs = (
        P("dp", "tensor"), P("dp"), P("dp", "tensor"), P("dp", "tensor"), P("dp", "tensor"),
        P(None, "tensor"), P(None, "tensor"), P("tensor", None),
    )
    out_specs = (P(None, "tensor", "dp"), P("tensor", "dp"), P("tensor", "dp"))
    return jax.shard_map(body, mesh=mesh, in_specs=in_specs, out_specs=out_specs, check_vma=False)
```

time: 1320 us -> 152 us (0.12)
  the two profiles are of different devices: /device:TPU:32 before, /device:TPU:1 now
where the time goes in v1:
time: 152 us
  Pallas kernels  144 us (95%)
  local copies, waits for them, and re-layouts  7.82 us (5%)
    pallas_call x1, Pallas kernels, body(): pl.pallas_call(functools.partial(kernel, dims), out_shape=jax.ShapeDtypeS...  144 us
    unnamed x12, local copies, waits for them, and re-layouts  6.59 us

profile of v1, /device:TPU:1, one launch (start us, length us, event | category | flops | bytes accessed | tf_op | source)
XLA Modules:
  0.0 152.0 jit_solution(5417960982359012620)
XLA Ops:
  0.6 0.0 copy-start
  0.6 1.6 %copy-done = bf16[8192,128]{1,0:T(8,128)(2,1)S(1)} copy-done((bf16[8192,128]{1,0:T(8,128)(2,1)S(1)}, bf16[8192,128]{1,0:T(8,128)(2,1)}, u32[]{:S(2)}) %copy-start) | copy-done | bytes 2097176
  2.2 0.0 copy-start.1
  2.2 1.2 copy-done.1
  3.5 0.0 copy-start.2
  3.5 1.0 copy-done.2
  4.5 0.0 copy-start.3
  4.5 1.0 copy-done.3
  5.5 0.0 copy-start.4
  5.5 1.0 copy-done.4
  6.6 0.0 copy-start.5
  6.6 0.7 copy-done.5
  7.2 143.6 %shard_map.103 = f32[160,128]{1,0:T(8,128)S(1)} custom-call(bf16[128,4096]{1,0:T(8,128)(2,1)S(1)} %copy-done.1, s32[1,128]{1,0:T(1,128)S(1)} %bitcast.9, bf16[128,2048]{1,0:T(8,128)(2,1)S(1)} %copy-done.2, bf16[128,2048]{1,0:T(8,128)(2,1)S(1)} %copy-done.3, bf16[128,2048]{1,0:T(8,128)(2,1)S(1)} %copy-done.4, bf16[8192,128]{1,0:T(8,128)(2,1)S(1)} %copy-done, ...), custom_call_target="tpu_custom_call" | custom-call | tf_op jit(solution)/shard_map/pallas_call | solution.py:538
  150.8 0.6 slice_bitcast_fusion
  151.4 0.6 slice_bitcast_fusion.2
Async XLA Ops:
  0.6 1.6 %copy-start = (bf16[8192,128]{1,0:T(8,128)(2,1)S(1)}, bf16[8192,128]{1,0:T(8,128)(2,1)}, u32[]{:S(2)}) copy-start(bf16[8192,128]{1,0:T(8,128)(2,1)} %gate.1) | copy-start | bytes 6291460
  2.2 1.2 copy-start.1
  3.5 1.0 copy-start.2
  4.5 1.0 copy-start.3
  5.5 1.0 copy-start.4
  6.6 0.7 copy-start.5

commit v2 on v0

v2 whole, which is shorter than its diff:
```python
import functools

import jax
import jax.numpy as jnp
from jax import lax
from jax.experimental import pallas as pl
from jax.experimental.pallas import tpu as pltpu
from jax.sharding import PartitionSpec as P

MESH = pl.DeviceIdType.MESH
BF = jnp.bfloat16
F32 = jnp.float32
NC = 2
NZ = 4
HALVES = 2
VMEM_LIMIT = 62 * 1024 * 1024


def sizes(mesh, pb):
    nt = mesh.shape["tensor"]
    return dict(NY=nt, NX=mesh.shape["dp"] // (nt * NZ * NC), NT=nt, PB=pb)


def kernel(
    dims, teacher, rowmap, student, projected, mlp, gate, up, down, out,
    Xs, stu, prj, err, wgu, WdS, TAy, TAx, XAy, XAx, GEy, GEx, pre, actp, actr, eb,
    RM, S0, S1, S2, msg1, msg2, RB1, RB2, fin, RB3,
    ld, z_s, z_r, wd_s, wd_r, eb_s, eb_r, rm_s, rm_r, rp_s, rp_r, ea_s, ea_r, ez_s, ez_r, ez_l,
    xa_s, xa_r, ta_s, ta_r, act_s, act_r, e_s, e_r, g_s, g_r, r1_s, r1_r, r2_s, r2_r, rb_s, rb_r,
):
    NY, NX, NT, PB = (dims[k] for k in ("NY", "NX", "NT", "PB"))
    NS = NY // NC
    TOK, S = mlp.shape
    H = gate.shape[1]
    DP = NY * NZ * NX * NC
    DTs = teacher.shape[1]
    ZW, ZT = S // NZ, DTs // (NY * NZ)
    L, LT = ZW // NX, ZT // NX
    R, RP = L // NC, LT // NC
    ROWS = 2 * R + RP
    NB = NY * NC * NX
    d = lax.axis_index("dp")
    t = lax.axis_index("tensor")
    c = lax.rem(d, NC)
    x = lax.rem(lax.div(d, NC), NX)
    zh = lax.rem(lax.div(d, NC * NX), NZ)
    y = lax.div(d, NC * NX * NZ)
    b = (y * NC + c) * NX + x
    factor = float(TOK * DP) ** -0.5
    shift = TOK.bit_length() - 1
    drains = []

    def did(y_, zh_, x_, c_, t_):
        return (((y_ * NZ + zh_) * NX + x_) * NC + c_, t_)

    def start(src, dst, ssem, rsem, where):
        copy = pltpu.make_async_remote_copy(
            src_ref=src, dst_ref=dst, send_sem=ssem, recv_sem=rsem, device_id=where, device_id_type=MESH
        )
        copy.start()
        return copy

    def send(src, dst, ssem, rsem, where):
        drains.append(start(src, dst, ssem, rsem, where))

    def send_if(cond, src, dst, ssem, rsem, where):
        @pl.when(cond)
        def _():
            start(src(), dst(), ssem, rsem, where)

    def arrived(ref, sem):
        pltpu.make_async_copy(ref, ref, sem).wait()

    def copy_or_send(own, src, dst, ssem, rsem, where):
        @pl.when(own)
        def _():
            pltpu.make_async_copy(src, dst, rsem).start()

        @pl.when(jnp.logical_not(own))
        def _():
            start(src, dst, ssem, rsem, where)

    def al(v, m):
        return pl.multiple_of(v, m)

    def plane(fn):
        def one(q, carry):
            fn(q, lax.div(q, NX * NC), lax.rem(q, NX), lax.rem(lax.div(q, NX), NC))
            return carry

        lax.fori_loop(0, NB, one, 0)

    half = TOK // HALVES

    def rows_of(h):
        return pl.ds(h * half, half)

    loads = [
        pltpu.make_async_copy(rowmap, RM.at[b, zh], ld.at[0]),
        pltpu.make_async_copy(student, stu, ld.at[1]),
        pltpu.make_async_copy(projected, prj, ld.at[2]),
        pltpu.make_async_copy(mlp, Xs.at[t], ld.at[3]),
        pltpu.make_async_copy(down.at[:, pl.ds(al(t * S, S), S)], WdS.at[t], ld.at[4]),
        pltpu.make_async_copy(gate, wgu.at[:, pl.ds(0, H)], ld.at[5]),
        pltpu.make_async_copy(up, wgu.at[:, pl.ds(H, H)], ld.at[6]),
    ]
    for copy in loads:
        copy.start()

    to_z = NC + lax.div(x * NC, NX)
    to_x = lax.rem(x * NC, NX) + c
    blk = (zh - NC) * NX + x
    from_x = jnp.where(zh < NC, x, lax.div(blk, NC))
    from_c = jnp.where(zh < NC, zh, lax.rem(blk, NC))

    barrier = pltpu.get_barrier_semaphore()

    def greet(where):
        pl.semaphore_signal(barrier, inc=1, device_id=where, device_id_type=MESH)

    def greet_plane(q, q_y, q_x, q_c):
        @pl.when(q != b)
        def _():
            greet(did(q_y, zh, q_x, q_c, t))

    plane(greet_plane)
    for o in range(1, NZ):
        greet(did(y, lax.rem(zh + o, NZ), x, c, t))
    for o in range(1, NT):
        greet((d, lax.rem(t + o, NT)))
    for q in range(NZ):
        @pl.when(jnp.logical_not((q == zh) & (from_x == x) & (from_c == c)))
        def _():
            greet(did(y, q, from_x, from_c, t))
    to_self = (c == zh) | ((to_z == zh) & (to_x == x))
    pl.semaphore_wait(barrier, NB - 1 + NZ - 1 + NT - 1 + 2 * NC - jnp.where(to_self, 1, 0))

    def z_send(k, h):
        sr, sl = t - k, t + k
        rows = rows_of(h)
        src_r = (lambda: mlp.at[rows]) if k == 0 else (lambda: Xs.at[sr, rows])
        src_l = (lambda: mlp.at[rows]) if k == 0 else (lambda: Xs.at[sl, rows])
        send_if((sr >= 0) & (t < NT - 1), src_r, lambda: Xs.at[sr, rows], z_s.at[0, k, h], z_r.at[0, k, h], (d, t + 1))
        send_if((sl <= NT - 1) & (t > 0), src_l, lambda: Xs.at[sl, rows], z_s.at[1, k, h], z_r.at[1, k, h], (d, t - 1))

    def z_drain(k, h):
        sr, sl = t - k, t + k

        @pl.when((sr >= 0) & (t < NT - 1))
        def _():
            arrived(Xs.at[sr, rows_of(h)], z_s.at[0, k, h])

        @pl.when((sl <= NT - 1) & (t > 0))
        def _():
            arrived(Xs.at[sl, rows_of(h)], z_s.at[1, k, h])

    def z_wait(k, h):
        @pl.when(t - k - 1 >= 0)
        def _():
            arrived(Xs.at[t - k - 1, rows_of(h)], z_r.at[0, k, h])

        @pl.when(t + k + 1 <= NT - 1)
        def _():
            arrived(Xs.at[t + k + 1, rows_of(h)], z_r.at[1, k, h])

    yrow = pl.ds(al((y * NC + c) * TOK, TOK), TOK)
    xrow = pl.ds(al((x * NC + c) * TOK, TOK), TOK)

    def a2a(s):
        for q_c in range(NC):
            copy_or_send(
                (s == y) & (q_c == c), Xs.at[s, :, pl.ds(q_c * ZW, ZW)], XAy.at[yrow], xa_s.at[0], xa_r.at[0],
                did(s, zh, x, q_c, t),
            )
        q_c = lax.div(s, NS)
        lane = pl.ds(al(lax.rem(s, NS) * NC * L, NC * L), NC * L)

        def one(q, carry):
            src = Xs.at[s, :, pl.ds(al((NX + q) * NC * L, NC * L), NC * L)]
            copy_or_send((q == x) & (q_c == c), src, XAx.at[xrow, lane], xa_s.at[1], xa_r.at[1], did(y, zh, q, q_c, t))
            return carry

        lax.fori_loop(0, NX, one, 0)

    def add_pre(s):
        pre[...] += jnp.dot(Xs[s], wgu[pl.ds(al(s * S, S), S), :], preferred_element_type=F32)

    def z_pass(k):
        for h in range(HALVES):
            z_wait(k, h)
            if k + 1 < NT - 1:
                z_send(k + 1, h)

        @pl.when(t - k - 1 >= 0)
        def _():
            a2a(t - k - 1)

        @pl.when(t + k + 1 <= NT - 1)
        def _():
            a2a(t + k + 1)

    def z_dot(k):
        @pl.when(t - k - 1 >= 0)
        def _():
            add_pre(t - k - 1)

        @pl.when(t + k + 1 <= NT - 1)
        def _():
            add_pre(t + k + 1)

    for h in range(HALVES):
        z_send(0, h)

    HR = H // (NX * NC)
    wrow = pl.ds(al((c * NX + x) * HR, HR), HR)
    crow = pl.ds(al(c * NX * HR, NX * HR), NX * HR)
    orow = pl.ds(al((1 - c) * NX * HR, NX * HR), NX * HR)
    for o in range(1, NT):
        p = lax.rem(t + o, NT)
        send(down.at[wrow, pl.ds(al(p * S, S), S)], WdS.at[t, wrow], wd_s.at[0, o - 1], wd_r.at[0, o - 1], (d, p))

    loads[0].wait()
    for o in range(1, NZ):
        q = lax.rem(zh + o, NZ)
        send(RM.at[b, zh], RM.at[b, zh], rm_s.at[o - 1], rm_r.at[o - 1], did(y, q, x, c, t))

    loads[1].wait()
    loads[2].wait()

    def err_rows(i, carry):
        r = pl.ds(al(i * 16, 16), 16)
        err[r, :] = ((stu[r, :].astype(F32) - prj[r, :].astype(F32)) * factor).astype(BF)
        return carry

    lax.fori_loop(0, TOK // 16, err_rows, 0)

    @pl.when(t == 0)
    def _():
        eb[...] = err[:, 0:PB]

    for o in range(1, NT):
        send_if(t == 0, lambda: eb, lambda: eb, eb_s.at[o - 1], eb_r, (d, o))

    for o in range(1, NZ):
        arrived(RM.at[b, lax.rem(zh + NZ - o, NZ)], rm_r.at[o - 1])

    def rm_out(q, q_y, q_x, q_c):
        @pl.when(q != b)
        def _():
            start(RM.at[b], RM.at[b], rp_s, rp_r, did(q_y, zh, q_x, q_c, t))

    plane(rm_out)

    for o in range(1, NT):
        p = lax.rem(t + NT - o, NT)
        arrived(WdS.at[p, wrow], wd_r.at[0, o - 1])
        for u in range(1, NX):
            send(
                WdS.at[p, wrow], WdS.at[p, wrow], wd_s.at[1, o - 1], wd_r.at[1, (o - 1) * (NX - 1) + u - 1],
                did(y, zh, lax.rem(x + u, NX), c, t),
            )

    loads[3].wait()
    a2a(t)

    loads[5].wait()
    loads[6].wait()
    pre[...] = jnp.dot(Xs[t], wgu[pl.ds(al(t * S, S), S), :], preferred_element_type=F32)

    if NT > 1:
        z_pass(0)

    arrived(RM.at[pl.ds(0, NB - 1)], rp_r)

    @pl.when(t != 0)
    def _():
        arrived(eb, eb_r)

    ids = RM[...].reshape(DP, TOK)
    slot = jnp.sum(jnp.where((ids >> shift) == d, ids & (TOK - 1), 0), axis=1, keepdims=True)
    pick = (lax.broadcasted_iota(jnp.int32, (DP, TOK), 1) == slot).astype(F32).astype(BF)
    S0[...] = jnp.dot(pick, eb[...], preferred_element_type=F32).reshape(S0.shape)

    def ea_out(q, q_y, q_x, q_c):
        copy_or_send(q == b, S0.at[q], S1.at[b], ea_s, ea_r, did(q_y, zh, q_x, q_c, t))

    plane(ea_out)

    for o in range(1, NT):
        p = lax.rem(t + NT - o, NT)
        for u in range(1, NX):
            r = pl.ds(al((c * NX + lax.rem(x + NX - u, NX)) * HR, HR), HR)
            arrived(WdS.at[p, r], wd_r.at[1, (o - 1) * (NX - 1) + u - 1])
        send(WdS.at[p, crow], WdS.at[p, crow], wd_s.at[2, o - 1], wd_r.at[2, o - 1], did(y, zh, x, 1 - c, t))

    if NT > 1:
        z_dot(0)
    if NT > 2:
        z_pass(1)

    arrived(S1, ea_r)
    keep = pltpu.make_async_copy(S1.at[:, zh], S2.at[:, zh], ez_l)
    keep.start()
    for o in range(1, NZ):
        q = lax.rem(zh + o, NZ)
        send(S1.at[:, q], S2.at[:, zh], ez_s.at[o - 1], ez_r.at[o - 1], did(y, q, x, c, t))

    loads[4].wait()
    for o in range(1, NT):
        p = lax.rem(t + NT - o, NT)
        arrived(WdS.at[p, orow], wd_r.at[2, o - 1])
    for p in range(NT):
        actp[p] = lax.dot_general(err[...], WdS[p], (((1,), (1,)), ((), ())), preferred_element_type=F32)
    for o in range(1, NT):
        p = lax.rem(t + o, NT)
        send(actp.at[p], actr.at[o - 1], act_s.at[o - 1], act_r.at[o - 1], (d, p))

    def tea_y(q, carry):
        q_y, q_c = lax.div(q, NC), lax.rem(q, NC)
        src = teacher.at[:, pl.ds(al((q_y * NZ + q_c) * ZT, ZT), ZT)]
        copy_or_send((q_y == y) & (q_c == c), src, TAy.at[yrow], ta_s.at[0], ta_r.at[0], did(q_y, zh, x, q_c, t))
        return carry

    def tea_x(q, carry):
        s, q_x = lax.div(q, NX), lax.rem(q, NX)
        q_c = lax.div(s, NS)
        src = teacher.at[:, pl.ds(al(((s * NZ + NC) * NX + q_x * NC) * LT, NC * LT), NC * LT)]
        dst = TAx.at[xrow, pl.ds(al(lax.rem(s, NS) * NC * LT, NC * LT), NC * LT)]
        copy_or_send((q_x == x) & (q_c == c), src, dst, ta_s.at[1], ta_r.at[1], did(y, zh, q_x, q_c, t))
        return carry

    lax.fori_loop(0, NY * NC, tea_y, 0)
    lax.fori_loop(0, NY * NX, tea_x, 0)

    if NT > 2:
        z_dot(1)
    if NT > 3:
        z_pass(2)

    keep.wait()
    for o in range(1, NZ):
        arrived(S2.at[:, lax.rem(zh + NZ - o, NZ)], ez_r.at[o - 1])
    row = lax.broadcasted_iota(jnp.int32, (DP, 1), 0)
    row_z, row_b = lax.rem(row, NZ), lax.div(row, NZ)
    row_x, row_c, row_y = lax.rem(row_b, NX), lax.rem(lax.div(row_b, NX), NC), lax.div(row_b, NX * NC)
    row_d = ((row_y * NZ + row_z) * NX + row_x) * NC + row_c
    order = ((RM[b, zh] >> shift) == row_d).astype(F32).astype(BF)
    sorted_err = lax.dot_general(
        S2[...].reshape(DP, PB).astype(BF), order, (((0,), (0,)), ((), ())), preferred_element_type=F32
    ).astype(BF)
    hid, proj_rows = pl.ds(0, 2 * H), pl.ds(2 * H, PB)
    GEy[proj_rows, yrow] = sorted_err
    GEx[proj_rows, xrow] = sorted_err

    def spread(rows, ssem, rsem):
        for q_c in range(NC):
            for o in range(1, NX):
                send(GEx.at[rows, xrow], GEx.at[rows, xrow], ssem.at[1], rsem.at[1], did(y, zh, lax.rem(x + o, NX), q_c, t))
            for o in range(1, NY):
                send(GEy.at[rows, yrow], GEy.at[rows, yrow], ssem.at[0], rsem.at[0], did(lax.rem(y + o, NY), zh, x, q_c, t))
        send(GEx.at[rows, xrow], GEx.at[rows, xrow], ssem.at[1], rsem.at[1], did(y, zh, x, 1 - c, t))
        send(GEy.at[rows, yrow], GEy.at[rows, yrow], ssem.at[0], rsem.at[0], did(y, zh, x, 1 - c, t))

    spread(proj_rows, e_s, e_r)

    if NT > 3:
        z_dot(2)

    act = actp[t]
    for o in range(1, NT):
        arrived(actr.at[o - 1], act_r.at[o - 1])
        act = act + actr[o - 1]
    gate_pre, up_pre = pre[:, 0:H], pre[:, H : 2 * H]
    sig = jax.nn.sigmoid(gate_pre)
    gate_grad = jnp.transpose(act * up_pre * sig * (1.0 + gate_pre * (1.0 - sig))).astype(BF)
    up_grad = jnp.transpose(act * gate_pre * sig).astype(BF)
    for buf, at in ((GEx, xrow), (GEy, yrow)):
        buf[0:H, at] = gate_grad
        buf[H : 2 * H, at] = up_grad
    spread(hid, g_s, g_r)

    oy, ox = pl.ds(0, (NY * NC - 1) * TOK), pl.ds(0, (NX * NC - 1) * TOK)
    arrived(GEy.at[proj_rows, oy], e_r.at[0])
    arrived(GEx.at[proj_rows, ox], e_r.at[1])
    arrived(TAy, ta_r.at[0])
    arrived(TAx, ta_r.at[1])
    proj1 = jnp.transpose(jnp.dot(GEy[proj_rows, :], TAy[...], preferred_element_type=F32)).astype(BF)
    proj2 = jnp.transpose(jnp.dot(GEx[proj_rows, :], TAx[...], preferred_element_type=F32)).astype(BF)
    for q in range(NX):
        msg1[q, 2 * H : 2 * H + LT, :] = proj1[q * LT : (q + 1) * LT, :]
    for i in range(NS):
        for q_c in range(NC):
            at = (i * NC + q_c) * LT
            msg2[i, q_c, 2 * H : 2 * H + LT, :] = proj2[at : at + LT, :]

    arrived(XAx, xa_r.at[1])
    arrived(GEx.at[hid, ox], g_r.at[1])
    tot2 = jnp.dot(GEx[hid, :], XAx[...], preferred_element_type=F32)
    for i in range(NS):
        for q_c in range(NC):
            at = (i * NC + q_c) * L
            msg2[i, q_c, 0 : 2 * H, 0:L] = tot2[:, at : at + L].astype(BF)
            s = c * NS + i
            copy_or_send(
                (s == y) & (q_c == c), msg2.at[i, q_c], RB2.at[y], r2_s.at[i, q_c], r2_r.at[y], did(s, zh, x, q_c, t)
            )
    arrived(XAy, xa_r.at[0])
    arrived(GEy.at[hid, oy], g_r.at[0])
    tot1 = jnp.dot(GEy[hid, :], XAy[...], preferred_element_type=F32)
    for q in range(NX):
        msg1[q, 0 : 2 * H, 0:L] = tot1[:, q * L : (q + 1) * L].astype(BF)
        copy_or_send(q == x, msg1.at[q], RB1.at[x], r1_s.at[q], r1_r.at[x], did(y, zh, q, c, t))

    for kind, (buf, sem, count, where) in enumerate(
        ((RB2, r2_r, NY, lambda q_c: (to_z, to_x, q_c)), (RB1, r1_r, NX, lambda q_c: (c, x, q_c)))
    ):
        part = None
        for q in range(count):
            arrived(buf.at[q], sem.at[q])
            part = buf[q].astype(F32) if part is None else part + buf[q].astype(F32)
        feats = jnp.transpose(part[0 : 2 * H, 0:L])
        for q_c in range(NC):
            r = slice(q_c * R, (q_c + 1) * R)
            fin[kind, q_c, 0:R, :] = feats[r, 0:H].astype(BF)
            fin[kind, q_c, R : 2 * R, :] = feats[r, H : 2 * H].astype(BF)
            at = 2 * H + q_c * RP
            fin[kind, q_c, 2 * R : ROWS, :] = part[at : at + RP, :].astype(BF)
            q_z, q_x, _ = where(q_c)
            copy_or_send(
                (q_z == zh) & (q_x == x) & (q_c == c), fin.at[kind, q_c], RB3.at[zh], rb_s.at[kind, q_c], rb_r.at[zh],
                did(y, q_z, q_x, q_c, t),
            )
    result = None
    for q in range(NZ):
        arrived(RB3.at[q], rb_r.at[q])
        result = RB3[q].astype(F32) if result is None else result + RB3[q].astype(F32)
    out[...] = result

    def left(own, ref, sem):
        @pl.when(jnp.logical_not(own))
        def _():
            arrived(ref, sem)

    for copy in drains:
        copy.wait_send()
    for k in range(NT - 1):
        for h in range(HALVES):
            z_drain(k, h)
    for o in range(1, NT):
        left(t != 0, eb, eb_s.at[o - 1])
    for q in range(NX):
        left(q == x, msg1.at[q], r1_s.at[q])
    for q_c in range(NC):
        for i in range(NS):
            left((c * NS + i == y) & (q_c == c), msg2.at[i, q_c], r2_s.at[i, q_c])
        left((to_z == zh) & (to_x == x) & (q_c == c), fin.at[0, q_c], rb_s.at[0, q_c])
        left((c == zh) & (q_c == c), fin.at[1, q_c], rb_s.at[1, q_c])
    arrived(RM.at[pl.ds(0, NB - 1)], rp_s)
    arrived(S1.at[pl.ds(0, NB - 1)], ea_s)
    for ref, sem, count in ((XAy, xa_s, NY), (TAy, ta_s, NY)):
        arrived(ref.at[pl.ds(0, (count * NC - 1) * TOK)], sem.at[0])
    for ref, sem, count in ((XAx, xa_s, NX), (TAx, ta_s, NX)):
        arrived(ref.at[pl.ds(0, (count * NC - 1) * TOK)], sem.at[1])


def solution(mesh, pb=128):
    dims = sizes(mesh, pb)
    NY, NX, NT = (dims[k] for k in ("NY", "NX", "NT"))

    def body(teacher_rows, row_map, student_hidden, projected, mlp_input, gate_bucket, up_bucket, down_bucket):
        TOK, S = mlp_input.shape
        F, H = gate_bucket.shape
        DTs = teacher_rows.shape[1]
        NS = NY // NC
        ZW, ZT = S // NZ, DTs // (NY * NZ)
        L, LT = ZW // NX, ZT // NX
        R, RP = L // NC, LT // NC
        NB = NY * NC * NX
        ROWS, MSG = 2 * R + RP, 2 * H + LT
        V, D = pltpu.VMEM, pltpu.SemaphoreType.DMA
        K = NT - 1
        scratch = [
            V((NT, TOK, S), BF), V((TOK, S), BF), V((TOK, S), BF), V((TOK, S), BF),
            V((F, 2 * H), BF), V((NT, H, S), BF),
            V((NY * NC * TOK, ZT), BF), V((NX * NC * TOK, NS * NC * LT), BF),
            V((NY * NC * TOK, ZW), BF), V((NX * NC * TOK, NS * NC * L), BF),
            V((2 * H + pb, NY * NC * TOK), BF), V((2 * H + pb, NX * NC * TOK), BF),
            V((TOK, 2 * H), F32), V((NT, TOK, H), F32), V((K, TOK, H), F32), V((TOK, pb), BF),
            V((NB, NZ, 1, TOK), jnp.int32), V((NB, NZ, 1, pb), F32), V((NB, NZ, 1, pb), F32), V((NB, NZ, 1, pb), F32),
            V((NX, MSG, H), BF), V((NS, NC, MSG, H), BF), V((NX, MSG, H), BF), V((NY, MSG, H), BF),
            V((2, NC, ROWS, H), BF), V((NZ, ROWS, H), BF),
            D((7,)), D((2, K, HALVES)), D((2, K, HALVES)),
            D((3, K)), D((3, K * max(NX - 1, 1))),
            D((K,)), D,
            D((NZ - 1,)), D((NZ - 1,)), D, D, D, D, D((NZ - 1,)), D((NZ - 1,)), D,
            D((2,)), D((2,)), D((2,)), D((2,)),
            D((K,)), D((K,)),
            D((2,)), D((2,)), D((2,)), D((2,)),
            D((NX,)), D((NX,)), D((NS, NC)), D((NY,)), D((2, NC)), D((NZ,)),
        ]
        res = pl.pallas_call(
            functools.partial(kernel, dims),
            out_shape=jax.ShapeDtypeStruct((2 * R + RP, H), F32),
            in_specs=[pl.BlockSpec(memory_space=pl.ANY)] * 8,
            out_specs=pl.BlockSpec(memory_space=pltpu.VMEM),
            scratch_shapes=scratch,
            compiler_params=pltpu.CompilerParams(
                collective_id=0, has_side_effects=True, vmem_limit_bytes=VMEM_LIMIT
            ),
        )(teacher_rows, row_map.reshape(1, TOK), student_hidden, projected, mlp_input, gate_bucket, up_bucket, down_bucket)
        return res[2 * R :].T[:, None, :], res[:R].T, res[R : 2 * R].T

    in_specs = (
        P("dp", "tensor"), P("dp"), P("dp", "tensor"), P("dp", "tensor"), P("dp", "tensor"),
        P(None, "tensor"), P(None, "tensor"), P("tensor", None),
    )
    out_specs = (P(None, "tensor", "dp"), P("tensor", "dp"), P("tensor", "dp"))
    return jax.shard_map(body, mesh=mesh, in_specs=in_specs, out_specs=out_specs, check_vma=False)
```

time: 1320 us -> 112 us (0.08)
  the two profiles are of different devices: /device:TPU:32 before, /device:TPU:97 now
where the time goes in v2:
time: 112 us
  Pallas kernels  108 us (96%)
  local copies, waits for them, and re-layouts  2.73 us (2%)
    pallas_call x1, Pallas kernels, body(): pl.pallas_call(functools.partial(kernel, dims), out_shape=jax.ShapeDtypeS...  108 us

profile of v2, /device:TPU:97, one launch (start us, length us, event | category | flops | bytes accessed | tf_op | source)
XLA Modules:
  0.0 111.6 jit_solution(10813275024324926047)
XLA Ops:
  0.6 108.2 %shard_map.103 = f32[160,128]{1,0:T(8,128)} custom-call(bf16[128,4096]{1,0:T(8,128)(2,1)} %teacher.1, s32[1,128]{1,0:T(1,128)} %bitcast.9, bf16[128,2048]{1,0:T(8,128)(2,1)} %student.1, bf16[128,2048]{1,0:T(8,128)(2,1)} %projected.1, bf16[128,2048]{1,0:T(8,128)(2,1)} %mlp.1, bf16[8192,128]{1,0:T(8,128)(2,1)} %gate.1, bf16[8192,128]{1,0:T(8,128)(2,1)} %up.1, ...), custom_call_target="tpu_custom_call" | custom-call | tf_op jit(solution)/shard_map/pallas_call | solution.py:501
  108.8 1.4 %slice_bitcast_fusion = (f32[128,64]{0,1:T(8,128)}, f32[128,64]{0,1:T(8,128)}) fusion(f32[160,128]{1,0:T(8,128)} %shard_map.103), kind=kLoop, calls=%fused_computation | loop fusion | bytes 131072 | tf_op jit(solution)/shard_map/transpose | solution.py:511
  110.2 1.3 %slice_bitcast_fusion.2 = f32[128,1,32]{0,2,1:T(8,128)} fusion(f32[160,128]{1,0:T(8,128)} %shard_map.103), kind=kLoop, calls=%fused_computation.2 | loop fusion | bytes 32768 | tf_op jit(solution)/shard_map/broadcast_in_dim | solution.py:511

commit v3 on v2

v3 whole, which is shorter than its diff:
```python
import functools

import jax
import jax.numpy as jnp
from jax import lax
from jax.experimental import pallas as pl
from jax.experimental.pallas import tpu as pltpu
from jax.sharding import PartitionSpec as P

MESH = pl.DeviceIdType.MESH
BF = jnp.bfloat16
F32 = jnp.float32
NC = 2
NZ = 4
HALVES = 2
VMEM_LIMIT = 62 * 1024 * 1024


def sizes(mesh, pb):
    nt = mesh.shape["tensor"]
    return dict(NY=nt, NX=mesh.shape["dp"] // (nt * NZ * NC), NT=nt, PB=pb)


def kernel(
    dims, teacher, rowmap, student, projected, mlp, gate, up, down, out,
    Xs, stu, prj, err, wgu, WdS, TAy, XAy, XAx, GEy, GEx, pre, actp, actr, eb,
    RM, S0, S1, S2, S3, msg1, msg2, msgp, RB1, RB2, RBX, fin, finp, RB3, RBP,
    ld, z_s, z_r, wd_s, wd_r, eb_s, eb_r, rm_s, rm_r, ea_s, ea_r, ea_l,
    xa_s, xa_r, ta_s, ta_r, act_s, act_r, e_s, e_r, g_s, g_r, r1_s, r1_r, r2_s, r2_r, rq_s, rq_r, rb_s, rb_r, rp_s, rp_r,
):
    NY, NX, NT, PB = (dims[k] for k in ("NY", "NX", "NT", "PB"))
    NS = NY // NC
    TOK, S = mlp.shape
    H = gate.shape[1]
    DP = NY * NZ * NX * NC
    DTs = teacher.shape[1]
    ZW, ZT = S // NZ, DTs // (NY * NZ)
    L, LT = ZW // NX, ZT // NX
    R, RP = L // NC, LT // NC
    NP = NZ // NC
    d = lax.axis_index("dp")
    t = lax.axis_index("tensor")
    c = lax.rem(d, NC)
    x = lax.rem(lax.div(d, NC), NX)
    zh = lax.rem(lax.div(d, NC * NX), NZ)
    y = lax.div(d, NC * NX * NZ)
    factor = float(TOK * DP) ** -0.5
    shift = TOK.bit_length() - 1
    drains = []

    def did(y_, zh_, x_, c_, t_):
        return (((y_ * NZ + zh_) * NX + x_) * NC + c_, t_)

    def start(src, dst, ssem, rsem, where):
        copy = pltpu.make_async_remote_copy(
            src_ref=src, dst_ref=dst, send_sem=ssem, recv_sem=rsem, device_id=where, device_id_type=MESH
        )
        copy.start()
        return copy

    def send(src, dst, ssem, rsem, where):
        drains.append(start(src, dst, ssem, rsem, where))

    def send_if(cond, src, dst, ssem, rsem, where):
        @pl.when(cond)
        def _():
            start(src(), dst(), ssem, rsem, where)

    def arrived(ref, sem):
        pltpu.make_async_copy(ref, ref, sem).wait()

    def copy_or_send(own, src, dst, ssem, rsem, where):
        @pl.when(own)
        def _():
            pltpu.make_async_copy(src, dst, rsem).start()

        @pl.when(jnp.logical_not(own))
        def _():
            start(src, dst, ssem, rsem, where)

    def al(v, m):
        return pl.multiple_of(v, m)

    half = TOK // HALVES

    def rows_of(h):
        return pl.ds(h * half, half)

    loads = [
        pltpu.make_async_copy(rowmap, RM.at[y, zh, x, c], ld.at[0]),
        pltpu.make_async_copy(student, stu, ld.at[1]),
        pltpu.make_async_copy(projected, prj, ld.at[2]),
        pltpu.make_async_copy(mlp, Xs.at[t], ld.at[3]),
        pltpu.make_async_copy(down.at[:, pl.ds(al(t * S, S), S)], WdS.at[0], ld.at[4]),
        pltpu.make_async_copy(gate, wgu.at[:, pl.ds(0, H)], ld.at[5]),
        pltpu.make_async_copy(up, wgu.at[:, pl.ds(H, H)], ld.at[6]),
    ]
    for copy in loads:
        copy.start()

    to_z = NC + lax.div(x * NC, NX)
    to_x = lax.rem(x * NC, NX) + c
    blk = (zh - NC) * NX + x
    from_x = jnp.where(zh < NC, x, lax.div(blk, NC))
    from_c = jnp.where(zh < NC, zh, lax.rem(blk, NC))

    barrier = pltpu.get_barrier_semaphore()

    def greet(where):
        pl.semaphore_signal(barrier, inc=1, device_id=where, device_id_type=MESH)

    for q_c in range(NC):
        for o in range(1, NX):
            greet(did(y, zh, lax.rem(x + o, NX), q_c, t))
        for o in range(1, NY):
            greet(did(lax.rem(y + o, NY), zh, x, q_c, t))
    greet(did(y, zh, x, 1 - c, t))
    for o in range(1, NZ):
        greet(did(y, lax.rem(zh + o, NZ), x, c, t))
    for o in range(1, NT):
        greet((d, lax.rem(t + o, NT)))
    for q in range(NZ):
        @pl.when(jnp.logical_not((q == zh) & (from_x == x) & (from_c == c)))
        def _():
            greet(did(y, q, from_x, from_c, t))
        @pl.when(jnp.logical_not((q == zh) & (lax.div(zh, NP) == c)))
        def _():
            greet(did(y, q, x, lax.div(zh, NP), t))
    to_self = (c == zh) | ((to_z == zh) & (to_x == x))
    to_self_p = lax.div(zh, NP) == c
    pl.semaphore_wait(
        barrier,
        (NX - 1 + NY - 1) * NC + 1 + NZ - 1 + NT - 1 + 2 * NC + NP * NC
        - jnp.where(to_self, 1, 0) - jnp.where(to_self_p, 1, 0),
    )

    def z_send(k, h):
        sr, sl = t - k, t + k
        rows = rows_of(h)
        src_r = (lambda: mlp.at[rows]) if k == 0 else (lambda: Xs.at[sr, rows])
        src_l = (lambda: mlp.at[rows]) if k == 0 else (lambda: Xs.at[sl, rows])
        send_if((sr >= 0) & (t < NT - 1), src_r, lambda: Xs.at[sr, rows], z_s.at[0, k, h], z_r.at[0, k, h], (d, t + 1))
        send_if((sl <= NT - 1) & (t > 0), src_l, lambda: Xs.at[sl, rows], z_s.at[1, k, h], z_r.at[1, k, h], (d, t - 1))

    def z_drain(k, h):
        sr, sl = t - k, t + k

        @pl.when((sr >= 0) & (t < NT - 1))
        def _():
            arrived(Xs.at[sr, rows_of(h)], z_s.at[0, k, h])

        @pl.when((sl <= NT - 1) & (t > 0))
        def _():
            arrived(Xs.at[sl, rows_of(h)], z_s.at[1, k, h])

    def z_wait(k, h):
        @pl.when(t - k - 1 >= 0)
        def _():
            arrived(Xs.at[t - k - 1, rows_of(h)], z_r.at[0, k, h])

        @pl.when(t + k + 1 <= NT - 1)
        def _():
            arrived(Xs.at[t + k + 1, rows_of(h)], z_r.at[1, k, h])

    yrow = pl.ds(al((y * NC + c) * TOK, TOK), TOK)
    xrow = pl.ds(al((x * NC + c) * TOK, TOK), TOK)

    def a2a(s, at, rows):
        yrows = pl.ds(al((y * NC + c) * TOK + at, rows), rows)
        xrows = pl.ds(al((x * NC + c) * TOK + at, rows), rows)
        for q_c in range(NC):
            copy_or_send(
                (s == y) & (q_c == c), Xs.at[s, pl.ds(at, rows), pl.ds(q_c * ZW, ZW)], XAy.at[yrows],
                xa_s.at[0], xa_r.at[0], did(s, zh, x, q_c, t),
            )
        q_c = lax.div(s, NS)
        lane = pl.ds(al(lax.rem(s, NS) * NC * L, NC * L), NC * L)

        def one(q, carry):
            src = Xs.at[s, pl.ds(at, rows), pl.ds(al((NX + q) * NC * L, NC * L), NC * L)]
            copy_or_send((q == x) & (q_c == c), src, XAx.at[xrows, lane], xa_s.at[1], xa_r.at[1], did(y, zh, q, q_c, t))
            return carry

        lax.fori_loop(0, NX, one, 0)

    def add_pre(s, at, rows):
        r = pl.ds(at, rows)
        pre[r, :] += jnp.dot(Xs[s, r, :], wgu[pl.ds(al(s * S, S), S), :], preferred_element_type=F32)

    def z_each(k, fn, at=0, rows=TOK):
        @pl.when(t - k - 1 >= 0)
        def _():
            fn(t - k - 1, at, rows)

        @pl.when(t + k + 1 <= NT - 1)
        def _():
            fn(t + k + 1, at, rows)

    def z_pass(k, h):
        z_wait(k, h)
        if k + 1 < NT - 1:
            z_send(k + 1, h)

    HR = H // (NX * NC)
    wrow = pl.ds(al((c * NX + x) * HR, HR), HR)
    crow = pl.ds(al(c * NX * HR, NX * HR), NX * HR)
    orow = pl.ds(al((1 - c) * NX * HR, NX * HR), NX * HR)
    for o in range(1, NT):
        p = lax.rem(t + o, NT)
        send(
            down.at[wrow, pl.ds(al(p * S, S), S)], WdS.at[NT - o, wrow], wd_s.at[0, o - 1], wd_r.at[0, NT - o - 1], (d, p)
        )

    loads[0].wait()
    for o in range(1, NZ):
        q = lax.rem(zh + o, NZ)
        send(RM.at[y, zh, x, c], RM.at[y, zh, x, c], rm_s.at[0], rm_r.at[0, o - 1], did(y, q, x, c, t))

    z_send(0, 0)

    loads[1].wait()
    loads[2].wait()

    def err_rows(i, carry):
        r = pl.ds(al(i * 16, 16), 16)
        err[r, :] = ((stu[r, :].astype(F32) - prj[r, :].astype(F32)) * factor).astype(BF)
        return carry

    lax.fori_loop(0, TOK // 16, err_rows, 0)

    @pl.when(t == 0)
    def _():
        eb[...] = err[:, 0:PB]

    for o in range(1, NT):
        send_if(t == 0, lambda: eb, lambda: eb, eb_s.at[o - 1], eb_r, (d, o))

    for h in range(1, HALVES):
        z_send(0, h)

    LAST = NT - 2

    LAST = NT - 2

    def others(fn):
        for o in range(NX):
            for w in range(NC):
                if o + w > 0:
                    fn(o * NC + w - 1, o, w)

    loads[3].wait()

    loads[5].wait()
    loads[6].wait()
    pre[...] = jnp.dot(Xs[t], wgu[pl.ds(al(t * S, S), S), :], preferred_element_type=F32)

    for o in range(1, NZ):
        arrived(RM.at[y, lax.rem(zh + NZ - o, NZ), x, c], rm_r.at[0, o - 1])
    for o in range(1, NY):
        send(RM.at[y, :, x, c], RM.at[y, :, x, c], rm_s.at[1], rm_r.at[1, o - 1], did(lax.rem(y + o, NY), zh, x, c, t))

    if LAST > 0:
        z_pass(0, 0)

    for o in range(1, NY):
        arrived(RM.at[lax.rem(y + NY - o, NY), :, x, c], rm_r.at[1, o - 1])
    others(lambda i, o, w: send(
        RM.at[:, :, x, c], RM.at[:, :, x, c], rm_s.at[2], rm_r.at[2, i], did(y, zh, lax.rem(x + o, NX), lax.rem(c + w, NC), t)
    ))

    rest = pl.ds(1, NT - 1)
    for o in range(1, NT):
        arrived(WdS.at[o, wrow], wd_r.at[0, o - 1])
    for u in range(1, NX):
        send(WdS.at[rest, wrow], WdS.at[rest, wrow], wd_s.at[1, u - 1], wd_r.at[1, u - 1], did(y, zh, lax.rem(x + u, NX), c, t))

    a2a(t, 0, TOK)

    if LAST > 0:
        z_pass(0, 1)

    others(lambda i, o, w: arrived(RM.at[:, :, lax.rem(x + NX - o, NX), lax.rem(c + NC - w, NC)], rm_r.at[2, i]))

    @pl.when(t != 0)
    def _():
        arrived(eb, eb_r)

    ids = RM[...].reshape(DP, TOK)
    slot = jnp.sum(jnp.where((ids >> shift) == d, ids & (TOK - 1), 0), axis=1, keepdims=True)
    pick = (lax.broadcasted_iota(jnp.int32, (DP, TOK), 1) == slot).astype(F32).astype(BF)
    S0[...] = jnp.dot(pick, eb[...], preferred_element_type=F32).reshape(S0.shape)
    keep = [pltpu.make_async_copy(S0.at[:, :, x, c], S1.at[:, :, x, c], ea_l.at[0])]
    keep[0].start()

    def ea_out(i, o, w):
        q_x, q_c = lax.rem(x + o, NX), lax.rem(c + w, NC)
        send(S0.at[:, :, q_x, q_c], S1.at[:, :, x, c], ea_s.at[0], ea_r.at[0, i], did(y, zh, q_x, q_c, t))

    others(ea_out)

    if LAST > 0:
        z_each(0, a2a)
    if LAST > 1:
        z_pass(1, 0)

    keep[0].wait()
    others(lambda i, o, w: arrived(S1.at[:, :, lax.rem(x + NX - o, NX), lax.rem(c + NC - w, NC)], ea_r.at[0, i]))
    keep.append(pltpu.make_async_copy(S1.at[y], S2.at[y], ea_l.at[1]))
    keep[1].start()
    for o in range(1, NY):
        q = lax.rem(y + o, NY)
        send(S1.at[q], S2.at[y], ea_s.at[1], ea_r.at[1, o - 1], did(q, zh, x, c, t))

    def tea_y(q, carry):
        q_y, q_c = lax.div(q, NC), lax.rem(q, NC)
        src = teacher.at[:, pl.ds(al((q_y * NC + q_c) * NP * ZT, NP * ZT), NP * ZT)]
        copy_or_send((q_y == y) & (q_c == c), src, TAy.at[yrow], ta_s, ta_r, did(q_y, zh, x, q_c, t))
        return carry

    lax.fori_loop(0, NY * NC, tea_y, 0)

    if LAST > 0:
        z_each(0, add_pre)
    if LAST > 1:
        z_pass(1, 1)

    keep[1].wait()
    for o in range(1, NY):
        arrived(S2.at[lax.rem(y + NY - o, NY)], ea_r.at[1, o - 1])
    keep.append(pltpu.make_async_copy(S2.at[:, zh], S3.at[:, zh], ea_l.at[2]))
    keep[2].start()
    for o in range(1, NZ):
        q = lax.rem(zh + o, NZ)
        send(S2.at[:, q], S3.at[:, zh], ea_s.at[2], ea_r.at[2, o - 1], did(y, q, x, c, t))

    if LAST > 1:
        z_each(1, a2a)

    for u in range(1, NX):
        r = pl.ds(al((c * NX + lax.rem(x + NX - u, NX)) * HR, HR), HR)
        arrived(WdS.at[rest, r], wd_r.at[1, u - 1])
    send(WdS.at[rest, crow], WdS.at[rest, crow], wd_s.at[2, 0], wd_r.at[2, 0], did(y, zh, x, 1 - c, t))

    loads[4].wait()
    arrived(WdS.at[rest, orow], wd_r.at[2, 0])
    for k in range(NT):
        actp[k] = lax.dot_general(err[...], WdS[k], (((1,), (1,)), ((), ())), preferred_element_type=F32)
    for k in range(1, NT):
        send(actp.at[k], actr.at[k - 1], act_s.at[k - 1], act_r.at[k - 1], (d, lax.rem(t + k, NT)))

    if LAST > 1:
        z_each(1, add_pre)

    for h in range(HALVES):
        z_pass(LAST, h)
        z_each(LAST, a2a, h * half, half)
        z_each(LAST, add_pre, h * half, half)

    hid, proj_rows = pl.ds(0, 2 * H), pl.ds(2 * H, PB)

    def along_y(rows, ssem, rsem):
        block = GEy.at[rows, yrow]
        for q_c in range(NC):
            for o in range(1, NY):
                send(block, block, ssem, rsem, did(lax.rem(y + o, NY), zh, x, q_c, t))
        send(block, block, ssem, rsem, did(y, zh, x, 1 - c, t))

    def along_x(ssem, rsem):
        block = GEx.at[:, xrow]
        for q_c in range(NC):
            for o in range(1, NX):
                send(block, block, ssem, rsem, did(y, zh, lax.rem(x + o, NX), q_c, t))
        send(block, block, ssem, rsem, did(y, zh, x, 1 - c, t))

    act = actp[0]
    for o in range(1, NT):
        arrived(actr.at[o - 1], act_r.at[o - 1])
        act = act + actr[o - 1]
    gate_pre, up_pre = pre[:, 0:H], pre[:, H : 2 * H]
    sig = jax.nn.sigmoid(gate_pre)
    gate_grad = jnp.transpose(act * up_pre * sig * (1.0 + gate_pre * (1.0 - sig))).astype(BF)
    up_grad = jnp.transpose(act * gate_pre * sig).astype(BF)
    for buf, at in ((GEx, xrow), (GEy, yrow)):
        buf[0:H, at] = gate_grad
        buf[H : 2 * H, at] = up_grad
    along_x(g_s.at[1], g_r.at[1])
    along_y(hid, g_s.at[0], g_r.at[0])

    keep[2].wait()
    for o in range(1, NZ):
        arrived(S3.at[:, lax.rem(zh + NZ - o, NZ)], ea_r.at[2, o - 1])
    order = ((RM[y, zh, x, c] >> shift) == lax.broadcasted_iota(jnp.int32, (DP, 1), 0)).astype(F32).astype(BF)
    GEy[proj_rows, yrow] = lax.dot_general(
        S3[...].reshape(DP, PB).astype(BF), order, (((0,), (0,)), ((), ())), preferred_element_type=F32
    ).astype(BF)

    along_y(proj_rows, e_s, e_r)

    oy, ox = pl.ds(0, (NY * NC - 1) * TOK), pl.ds(0, (NX * NC - 1) * TOK)

    arrived(XAx, xa_r.at[1])
    arrived(GEx.at[:, ox], g_r.at[1])
    tot2 = jnp.dot(GEx[...], XAx[...], preferred_element_type=F32)
    for i in range(NS):
        for q_c in range(NC):
            at = (i * NC + q_c) * L
            msg2[i, q_c, :, 0:L] = tot2[:, at : at + L].astype(BF)
            s = c * NS + i
            copy_or_send(
                (s == y) & (q_c == c), msg2.at[i, q_c], RB2.at[y], r2_s.at[i, q_c], r2_r.at[y], did(s, zh, x, q_c, t)
            )
    arrived(XAy, xa_r.at[0])
    arrived(GEy.at[hid, oy], g_r.at[0])
    tot1 = jnp.dot(GEy[hid, :], XAy[...], preferred_element_type=F32)
    for q in range(NX):
        msg1[q, :, 0:L] = tot1[:, q * L : (q + 1) * L].astype(BF)
        copy_or_send(q == x, msg1.at[q], RB1.at[x], r1_s.at[q], r1_r.at[x], did(y, zh, q, c, t))

    arrived(GEy.at[proj_rows, oy], e_r)
    arrived(TAy, ta_r)
    proj = jnp.transpose(jnp.dot(GEy[proj_rows, :], TAy[...], preferred_element_type=F32)).astype(BF)
    for q in range(NX):
        for j in range(NP):
            at = j * ZT + q * LT
            msgp[q, j * LT : (j + 1) * LT, :] = proj[at : at + LT, :]
        copy_or_send(q == x, msgp.at[q], RBX.at[x], rq_s.at[q], rq_r.at[x], did(y, zh, q, c, t))

    for kind, (buf, sem, count, where) in enumerate(
        ((RB2, r2_r, NY, lambda q_c: (to_z, to_x, q_c)), (RB1, r1_r, NX, lambda q_c: (c, x, q_c)))
    ):
        part = None
        for q in range(count):
            arrived(buf.at[q], sem.at[q])
            part = buf[q].astype(F32) if part is None else part + buf[q].astype(F32)
        feats = jnp.transpose(part[:, 0:L])
        for q_c in range(NC):
            r = slice(q_c * R, (q_c + 1) * R)
            fin[kind, q_c, 0:R, :] = feats[r, 0:H].astype(BF)
            fin[kind, q_c, R : 2 * R, :] = feats[r, H : 2 * H].astype(BF)
            q_z, q_x, _ = where(q_c)
            copy_or_send(
                (q_z == zh) & (q_x == x) & (q_c == c), fin.at[kind, q_c], RB3.at[zh], rb_s.at[kind, q_c], rb_r.at[zh],
                did(y, q_z, q_x, q_c, t),
            )
    part = None
    for q in range(NX):
        arrived(RBX.at[q], rq_r.at[q])
        part = RBX[q].astype(F32) if part is None else part + RBX[q].astype(F32)
    for j in range(NP):
        for q_c in range(NC):
            at = j * LT + q_c * RP
            finp[j, q_c] = part[at : at + RP, :].astype(BF)
            q_z = c * NP + j
            copy_or_send(
                (q_z == zh) & (q_c == c), finp.at[j, q_c], RBP.at[zh], rp_s.at[j, q_c], rp_r.at[zh], did(y, q_z, x, q_c, t)
            )
    result = None
    for q in range(NZ):
        arrived(RB3.at[q], rb_r.at[q])
        result = RB3[q].astype(F32) if result is None else result + RB3[q].astype(F32)
    out[0 : 2 * R, :] = result
    result = None
    for q in range(NZ):
        arrived(RBP.at[q], rp_r.at[q])
        result = RBP[q].astype(F32) if result is None else result + RBP[q].astype(F32)
    out[2 * R : 2 * R + RP, :] = result

    def left(own, ref, sem):
        @pl.when(jnp.logical_not(own))
        def _():
            arrived(ref, sem)

    for copy in drains:
        copy.wait_send()
    for k in range(NT - 1):
        for h in range(HALVES):
            z_drain(k, h)
    for o in range(1, NT):
        left(t != 0, eb, eb_s.at[o - 1])
    for q in range(NX):
        left(q == x, msg1.at[q], r1_s.at[q])
        left(q == x, msgp.at[q], rq_s.at[q])
    for q_c in range(NC):
        for i in range(NS):
            left((c * NS + i == y) & (q_c == c), msg2.at[i, q_c], r2_s.at[i, q_c])
        left((to_z == zh) & (to_x == x) & (q_c == c), fin.at[0, q_c], rb_s.at[0, q_c])
        left((c == zh) & (q_c == c), fin.at[1, q_c], rb_s.at[1, q_c])
        for j in range(NP):
            left((c * NP + j == zh) & (q_c == c), finp.at[j, q_c], rp_s.at[j, q_c])
    arrived(XAy.at[pl.ds(0, (NY * NC - 1) * TOK)], xa_s.at[0])
    arrived(XAx.at[pl.ds(0, (NX * NC - 1) * TOK)], xa_s.at[1])
    arrived(TAy.at[pl.ds(0, (NY * NC - 1) * TOK)], ta_s)


def solution(mesh, pb=128):
    dims = sizes(mesh, pb)
    NY, NX, NT = (dims[k] for k in ("NY", "NX", "NT"))

    def body(teacher_rows, row_map, student_hidden, projected, mlp_input, gate_bucket, up_bucket, down_bucket):
        TOK, S = mlp_input.shape
        F, H = gate_bucket.shape
        DTs = teacher_rows.shape[1]
        NS = NY // NC
        ZW, ZT = S // NZ, DTs // (NY * NZ)
        L, LT = ZW // NX, ZT // NX
        R, RP = L // NC, LT // NC
        NP = NZ // NC
        rows5 = (NY, NZ, NX, NC, 1)
        V, D = pltpu.VMEM, pltpu.SemaphoreType.DMA
        K = NT - 1
        scratch = [
            V((NT, TOK, S), BF), V((TOK, S), BF), V((TOK, S), BF), V((TOK, S), BF),
            V((F, 2 * H), BF), V((NT, H, S), BF),
            V((NY * NC * TOK, NP * ZT), BF),
            V((NY * NC * TOK, ZW), BF), V((NX * NC * TOK, NS * NC * L), BF),
            V((2 * H + pb, NY * NC * TOK), BF), V((2 * H, NX * NC * TOK), BF),
            V((TOK, 2 * H), F32), V((NT, TOK, H), F32), V((K, TOK, H), F32), V((TOK, pb), BF),
            V((*rows5, TOK), jnp.int32), *[V((*rows5, pb), F32)] * 4,
            V((NX, 2 * H, H), BF), V((NS, NC, 2 * H, H), BF), V((NX, NP * LT, pb), BF),
            V((NX, 2 * H, H), BF), V((NY, 2 * H, H), BF), V((NX, NP * LT, pb), BF),
            V((2, NC, 2 * R, H), BF), V((NP, NC, RP, H), BF), V((NZ, 2 * R, H), BF), V((NZ, RP, H), BF),
            D((7,)), D((2, K, HALVES)), D((2, K, HALVES)),
            D((3, 3)), D((3, 3)),
            D((K,)), D,
            D((3,)), D((3, NX * NC)), D((3,)), D((3, NX * NC)), D((3,)),
            D((2,)), D((2,)), D, D,
            D((K,)), D((K,)),
            D, D, D((2,)), D((2,)),
            D((NX,)), D((NX,)), D((NS, NC)), D((NY,)), D((NX,)), D((NX,)), D((2, NC)), D((NZ,)), D((NP, NC)), D((NZ,)),
        ]
        res = pl.pallas_call(
            functools.partial(kernel, dims),
            out_shape=jax.ShapeDtypeStruct((2 * R + RP, H), F32),
            in_specs=[pl.BlockSpec(memory_space=pl.ANY)] * 8,
            out_specs=pl.BlockSpec(memory_space=pltpu.VMEM),
            scratch_shapes=scratch,
            compiler_params=pltpu.CompilerParams(
                collective_id=0, has_side_effects=True, vmem_limit_bytes=VMEM_LIMIT
            ),
        )(teacher_rows, row_map.reshape(1, TOK), student_hidden, projected, mlp_input, gate_bucket, up_bucket, down_bucket)
        return res[2 * R :].T[:, None, :], res[:R].T, res[R : 2 * R].T

    in_specs = (
        P("dp", "tensor"), P("dp"), P("dp", "tensor"), P("dp", "tensor"), P("dp", "tensor"),
        P(None, "tensor"), P(None, "tensor"), P("tensor", None),
    )
    out_specs = (P(None, "tensor", "dp"), P("tensor", "dp"), P("tensor", "dp"))
    return jax.shard_map(body, mesh=mesh, in_specs=in_specs, out_specs=out_specs, check_vma=False)
```

time: 112 us -> 100 us (0.89)
  the two profiles are of different devices: /device:TPU:97 before, /device:TPU:17 now
where the time goes in v3:
time: 100 us; the launch traced here: 99.9 us
  Pallas kernels  96.5 us (96%)
  local copies, waits for them, and re-layouts  2.73 us (3%)
    pallas_call x1, Pallas kernels, body(): pl.pallas_call(functools.partial(kernel, dims), out_shape=jax.ShapeDtypeS...  96.5 us

profile of v3, /device:TPU:17, one launch (start us, length us, event | category | flops | bytes accessed | tf_op | source)
XLA Modules:
  0.0 99.9 jit_solution(3643429544515849898)
XLA Ops:
  0.6 96.5 %shard_map.103 = f32[160,128]{1,0:T(8,128)} custom-call(bf16[128,4096]{1,0:T(8,128)(2,1)} %teacher.1, s32[1,128]{1,0:T(1,128)} %bitcast.9, bf16[128,2048]{1,0:T(8,128)(2,1)} %student.1, bf16[128,2048]{1,0:T(8,128)(2,1)} %projected.1, bf16[128,2048]{1,0:T(8,128)(2,1)} %mlp.1, bf16[8192,128]{1,0:T(8,128)(2,1)} %gate.1, bf16[8192,128]{1,0:T(8,128)(2,1)} %up.1, ...), custom_call_target="tpu_custom_call" | custom-call | tf_op jit(solution)/shard_map/pallas_call | solution.py:531
  97.2 1.4 %slice_bitcast_fusion = (f32[128,64]{0,1:T(8,128)}, f32[128,64]{0,1:T(8,128)}) fusion(f32[160,128]{1,0:T(8,128)} %shard_map.103), kind=kLoop, calls=%fused_computation | loop fusion | bytes 131072 | tf_op jit(solution)/shard_map/transpose | solution.py:541
  98.6 1.3 %slice_bitcast_fusion.2 = f32[128,1,32]{0,2,1:T(8,128)} fusion(f32[160,128]{1,0:T(8,128)} %shard_map.103), kind=kLoop, calls=%fused_computation.2 | loop fusion | bytes 32768 | tf_op jit(solution)/shard_map/broadcast_in_dim | solution.py:541

commit v4 on v3

--- a/solution.py
+++ b/solution.py
@@ -23,8 +23,8 @@
 
 def kernel(
     dims, teacher, rowmap, student, projected, mlp, gate, up, down, out,
-    Xs, stu, prj, err, wgu, WdS, TAy, XAy, XAx, GEy, GEx, pre, actp, actr, eb,
-    RM, S0, S1, S2, S3, msg1, msg2, msgp, RB1, RB2, RBX, fin, finp, RB3, RBP,
+    Xs, stu, prj, err, wgu, WdS, TAy, XAy, XAx, GEy, GEx, pre, actp, actr, eb, eb_in,
+    RM, S0, S1, S2, S3, S4, msg1, msg2, msgp, RB1, RB2, RBX, fin, finp, RB3, RBP,
     ld, z_s, z_r, wd_s, wd_r, eb_s, eb_r, rm_s, rm_r, ea_s, ea_r, ea_l,
     xa_s, xa_r, ta_s, ta_r, act_s, act_r, e_s, e_r, g_s, g_r, r1_s, r1_r, r2_s, r2_r, rq_s, rq_r, rb_s, rb_r, rp_s, rp_r,
 ):
@@ -94,8 +94,10 @@
         pltpu.make_async_copy(down.at[:, pl.ds(al(t * S, S), S)], WdS.at[0], ld.at[4]),
         pltpu.make_async_copy(gate, wgu.at[:, pl.ds(0, H)], ld.at[5]),
         pltpu.make_async_copy(up, wgu.at[:, pl.ds(H, H)], ld.at[6]),
+        pltpu.make_async_copy(student.at[:, pl.ds(0, PB)], eb_in.at[0], ld.at[7]),
+        pltpu.make_async_copy(projected.at[:, pl.ds(0, PB)], eb_in.at[1], ld.at[8]),
     ]
-    for copy in loads:
+    for copy in loads[7:] + loads[:7]:
         copy.start()
 
     to_z = NC + lax.div(x * NC, NX)
@@ -126,6 +128,13 @@
         @pl.when(jnp.logical_not((q == zh) & (lax.div(zh, NP) == c)))
         def _():
             greet(did(y, q, x, lax.div(zh, NP), t))
+    loads[7].wait()
+    loads[8].wait()
+
+    @pl.when(t == 0)
+    def _():
+        eb[...] = ((eb_in[0].astype(F32) - eb_in[1].astype(F32)) * factor).astype(BF)
+
     to_self = (c == zh) | ((to_z == zh) & (to_x == x))
     to_self_p = lax.div(zh, NP) == c
     pl.semaphore_wait(
@@ -201,22 +210,27 @@
         if k + 1 < NT - 1:
             z_send(k + 1, h)
 
-    HR = H // (NX * NC)
+    loads[0].wait()
+    for o in range(1, NZ):
+        q = lax.rem(zh + o, NZ)
+        send(RM.at[y, zh, x, c], RM.at[y, zh, x, c], rm_s.at[0], rm_r.at[0, o - 1], did(y, q, x, c, t))
+
+    for o in range(1, NT):
+        send_if(t == 0, lambda: eb, lambda: eb, eb_s.at[o - 1], eb_r, (d, o))
+
+    HR, SQ = H // (NX * NC), S // NY
+    ycols = pl.ds(al(y * SQ, SQ), SQ)
     wrow = pl.ds(al((c * NX + x) * HR, HR), HR)
     crow = pl.ds(al(c * NX * HR, NX * HR), NX * HR)
     orow = pl.ds(al((1 - c) * NX * HR, NX * HR), NX * HR)
     for o in range(1, NT):
         p = lax.rem(t + o, NT)
         send(
-            down.at[wrow, pl.ds(al(p * S, S), S)], WdS.at[NT - o, wrow], wd_s.at[0, o - 1], wd_r.at[0, NT - o - 1], (d, p)
+            down.at[wrow, pl.ds(al(p * S + y * SQ, SQ), SQ)], WdS.at[NT - o, wrow, ycols], wd_s.at[0, o - 1], wd_r.at[0, NT - o - 1], (d, p)
         )
 
-    loads[0].wait()
-    for o in range(1, NZ):
-        q = lax.rem(zh + o, NZ)
-        send(RM.at[y, zh, x, c], RM.at[y, zh, x, c], rm_s.at[0], rm_r.at[0, o - 1], did(y, q, x, c, t))
-
-    z_send(0, 0)
+    for h in range(HALVES):
+        z_send(0, h)
 
     loads[1].wait()
     loads[2].wait()
@@ -227,18 +241,6 @@
         return carry
 
     lax.fori_loop(0, TOK // 16, err_rows, 0)
-
-    @pl.when(t == 0)
-    def _():
-        eb[...] = err[:, 0:PB]
-
-    for o in range(1, NT):
-        send_if(t == 0, lambda: eb, lambda: eb, eb_s.at[o - 1], eb_r, (d, o))
-
-    for h in range(1, HALVES):
-        z_send(0, h)
-
-    LAST = NT - 2
 
     LAST = NT - 2
 
@@ -259,6 +261,23 @@
     for o in range(1, NY):
         send(RM.at[y, :, x, c], RM.at[y, :, x, c], rm_s.at[1], rm_r.at[1, o - 1], did(lax.rem(y + o, NY), zh, x, c, t))
 
+    rest = pl.ds(1, NT - 1)
+    for o in range(1, NT):
+        arrived(WdS.at[o, wrow, ycols], wd_r.at[0, o - 1])
+    for u in range(1, NY):
+        send(
+            WdS.at[rest, wrow, ycols], WdS.at[rest, wrow, ycols], wd_s.at[3, u - 1], wd_r.at[3, u - 1],
+            did(lax.rem(y + u, NY), zh, x, c, t),
+        )
+
+    def tea_y(q, carry):
+        q_y, q_c = lax.div(q, NC), lax.rem(q, NC)
+        src = teacher.at[:, pl.ds(al((q_y * NC + q_c) * NP * ZT, NP * ZT), NP * ZT)]
+        copy_or_send((q_y == y) & (q_c == c), src, TAy.at[yrow], ta_s, ta_r, did(q_y, zh, x, q_c, t))
+        return carry
+
+    lax.fori_loop(0, NY * NC, tea_y, 0)
+
     if LAST > 0:
         z_pass(0, 0)
 
@@ -268,9 +287,9 @@
         RM.at[:, :, x, c], RM.at[:, :, x, c], rm_s.at[2], rm_r.at[2, i], did(y, zh, lax.rem(x + o, NX), lax.rem(c + w, NC), t)
     ))
 
-    rest = pl.ds(1, NT - 1)
-    for o in range(1, NT):
-        arrived(WdS.at[o, wrow], wd_r.at[0, o - 1])
+    for u in range(1, NY):
+        cols = pl.ds(al(lax.rem(y + NY - u, NY) * SQ, SQ), SQ)
+        arrived(WdS.at[rest, wrow, cols], wd_r.at[3, u - 1])
     for u in range(1, NX):
         send(WdS.at[rest, wrow], WdS.at[rest, wrow], wd_s.at[1, u - 1], wd_r.at[1, u - 1], did(y, zh, lax.rem(x + u, NX), c, t))
 
@@ -311,31 +330,24 @@
         q = lax.rem(y + o, NY)
         send(S1.at[q], S2.at[y], ea_s.at[1], ea_r.at[1, o - 1], did(q, zh, x, c, t))
 
-    def tea_y(q, carry):
-        q_y, q_c = lax.div(q, NC), lax.rem(q, NC)
-        src = teacher.at[:, pl.ds(al((q_y * NC + q_c) * NP * ZT, NP * ZT), NP * ZT)]
-        copy_or_send((q_y == y) & (q_c == c), src, TAy.at[yrow], ta_s, ta_r, did(q_y, zh, x, q_c, t))
-        return carry
-
-    lax.fori_loop(0, NY * NC, tea_y, 0)
-
-    if LAST > 0:
-        z_each(0, add_pre)
     if LAST > 1:
         z_pass(1, 1)
+
+    if LAST > 1:
+        z_each(1, a2a)
 
     keep[1].wait()
     for o in range(1, NY):
         arrived(S2.at[lax.rem(y + NY - o, NY)], ea_r.at[1, o - 1])
-    keep.append(pltpu.make_async_copy(S2.at[:, zh], S3.at[:, zh], ea_l.at[2]))
-    keep[2].start()
+    for q in range(NZ):
+        S3[q] = S2[:, q].reshape(DP // NZ, PB).astype(BF)
     for o in range(1, NZ):
         q = lax.rem(zh + o, NZ)
-        send(S2.at[:, q], S3.at[:, zh], ea_s.at[2], ea_r.at[2, o - 1], did(y, q, x, c, t))
-
-    if LAST > 1:
-        z_each(1, a2a)
-
+        send(S3.at[q], S4.at[zh], ea_s.at[2], ea_r.at[2, o - 1], did(y, q, x, c, t))
+    S4[zh] = S3[zh]
+
+    if LAST > 0:
+        z_each(0, add_pre)
     for u in range(1, NX):
         r = pl.ds(al((c * NX + lax.rem(x + NX - u, NX)) * HR, HR), HR)
         arrived(WdS.at[rest, r], wd_r.at[1, u - 1])
@@ -351,11 +363,6 @@
     if LAST > 1:
         z_each(1, add_pre)
 
-    for h in range(HALVES):
-        z_pass(LAST, h)
-        z_each(LAST, a2a, h * half, half)
-        z_each(LAST, add_pre, h * half, half)
-
     hid, proj_rows = pl.ds(0, 2 * H), pl.ds(2 * H, PB)
 
     def along_y(rows, ssem, rsem):
@@ -371,6 +378,28 @@
             for o in range(1, NX):
                 send(block, block, ssem, rsem, did(y, zh, lax.rem(x + o, NX), q_c, t))
         send(block, block, ssem, rsem, did(y, zh, x, 1 - c, t))
+
+    def z_last(h):
+        z_pass(LAST, h)
+        z_each(LAST, a2a, h * half, half)
+        z_each(LAST, add_pre, h * half, half)
+
+    z_last(0)
+
+    for o in range(1, NZ):
+        arrived(S4.at[lax.rem(zh + NZ - o, NZ)], ea_r.at[2, o - 1])
+    row = lax.broadcasted_iota(jnp.int32, (DP, 1), 0)
+    group, place = lax.div(row, DP // NZ), lax.rem(row, DP // NZ)
+    row_d = (lax.div(place, NX * NC) * NZ + group) * (NX * NC) + lax.rem(place, NX * NC)
+    order = ((RM[y, zh, x, c] >> shift) == row_d).astype(F32).astype(BF)
+    GEy[proj_rows, yrow] = lax.dot_general(
+        S4[...].reshape(DP, PB), order, (((0,), (0,)), ((), ())), preferred_element_type=F32
+    ).astype(BF)
+
+    along_y(proj_rows, e_s, e_r)
+
+    for h in range(1, HALVES):
+        z_last(h)
 
     act = actp[0]
     for o in range(1, NT):
@@ -386,17 +415,16 @@
     along_x(g_s.at[1], g_r.at[1])
     along_y(hid, g_s.at[0], g_r.at[0])
 
-    keep[2].wait()
-    for o in range(1, NZ):
-        arrived(S3.at[:, lax.rem(zh + NZ - o, NZ)], ea_r.at[2, o - 1])
-    order = ((RM[y, zh, x, c] >> shift) == lax.broadcasted_iota(jnp.int32, (DP, 1), 0)).astype(F32).astype(BF)
-    GEy[proj_rows, yrow] = lax.dot_general(
-        S3[...].reshape(DP, PB).astype(BF), order, (((0,), (0,)), ((), ())), preferred_element_type=F32
-    ).astype(BF)
-
-    along_y(proj_rows, e_s, e_r)
-
     oy, ox = pl.ds(0, (NY * NC - 1) * TOK), pl.ds(0, (NX * NC - 1) * TOK)
+
+    arrived(GEy.at[proj_rows, oy], e_r)
+    arrived(TAy, ta_r)
+    proj = jnp.transpose(jnp.dot(GEy[proj_rows, :], TAy[...], preferred_element_type=F32)).astype(BF)
+    for q in range(NX):
+        for j in range(NP):
+            at = j * ZT + q * LT
+            msgp[q, j * LT : (j + 1) * LT, :] = proj[at : at + LT, :]
+        copy_or_send(q == x, msgp.at[q], RBX.at[x], rq_s.at[q], rq_r.at[x], did(y, zh, q, c, t))
 
     arrived(XAx, xa_r.at[1])
     arrived(GEx.at[:, ox], g_r.at[1])
@@ -416,15 +444,18 @@
         msg1[q, :, 0:L] = tot1[:, q * L : (q + 1) * L].astype(BF)
         copy_or_send(q == x, msg1.at[q], RB1.at[x], r1_s.at[q], r1_r.at[x], did(y, zh, q, c, t))
 
-    arrived(GEy.at[proj_rows, oy], e_r)
-    arrived(TAy, ta_r)
-    proj = jnp.transpose(jnp.dot(GEy[proj_rows, :], TAy[...], preferred_element_type=F32)).astype(BF)
+    part = None
     for q in range(NX):
-        for j in range(NP):
-            at = j * ZT + q * LT
-            msgp[q, j * LT : (j + 1) * LT, :] = proj[at : at + LT, :]
-        copy_or_send(q == x, msgp.at[q], RBX.at[x], rq_s.at[q], rq_r.at[x], did(y, zh, q, c, t))
-
+        arrived(RBX.at[q], rq_r.at[q])
+        part = RBX[q].astype(F32) if part is None else part + RBX[q].astype(F32)
+    for j in range(NP):
+        for q_c in range(NC):
+            at = j * LT + q_c * RP
+            finp[j, q_c] = part[at : at + RP, :].astype(BF)
+            q_z = c * NP + j
+            copy_or_send(
+                (q_z == zh) & (q_c == c), finp.at[j, q_c], RBP.at[zh], rp_s.at[j, q_c], rp_r.at[zh], did(y, q_z, x, q_c, t)
+            )
     for kind, (buf, sem, count, where) in enumerate(
         ((RB2, r2_r, NY, lambda q_c: (to_z, to_x, q_c)), (RB1, r1_r, NX, lambda q_c: (c, x, q_c)))
     ):
@@ -441,18 +472,6 @@
             copy_or_send(
                 (q_z == zh) & (q_x == x) & (q_c == c), fin.at[kind, q_c], RB3.at[zh], rb_s.at[kind, q_c], rb_r.at[zh],
                 did(y, q_z, q_x, q_c, t),
-            )
-    part = None
-    for q in range(NX):
-        arrived(RBX.at[q], rq_r.at[q])
-        part = RBX[q].astype(F32) if part is None else part + RBX[q].astype(F32)
-    for j in range(NP):
-        for q_c in range(NC):
-            at = j * LT + q_c * RP
-            finp[j, q_c] = part[at : at + RP, :].astype(BF)
-            q_z = c * NP + j
-            copy_or_send(
-                (q_z == zh) & (q_c == c), finp.at[j, q_c], RBP.at[zh], rp_s.at[j, q_c], rp_r.at[zh], did(y, q_z, x, q_c, t)
             )
     result = None
     for q in range(NZ):
@@ -514,13 +533,14 @@
             V((NY * NC * TOK, NP * ZT), BF),
             V((NY * NC * TOK, ZW), BF), V((NX * NC * TOK, NS * NC * L), BF),
             V((2 * H + pb, NY * NC * TOK), BF), V((2 * H, NX * NC * TOK), BF),
-            V((TOK, 2 * H), F32), V((NT, TOK, H), F32), V((K, TOK, H), F32), V((TOK, pb), BF),
-            V((*rows5, TOK), jnp.int32), *[V((*rows5, pb), F32)] * 4,
+            V((TOK, 2 * H), F32), V((NT, TOK, H), F32), V((K, TOK, H), F32), V((TOK, pb), BF), V((2, TOK, pb), BF),
+            V((*rows5, TOK), jnp.int32), *[V((*rows5, pb), F32)] * 3,
+            *[V((NZ, NY * NX * NC, pb), BF)] * 2,
             V((NX, 2 * H, H), BF), V((NS, NC, 2 * H, H), BF), V((NX, NP * LT, pb), BF),
             V((NX, 2 * H, H), BF), V((NY, 2 * H, H), BF), V((NX, NP * LT, pb), BF),
             V((2, NC, 2 * R, H), BF), V((NP, NC, RP, H), BF), V((NZ, 2 * R, H), BF), V((NZ, RP, H), BF),
-            D((7,)), D((2, K, HALVES)), D((2, K, HALVES)),
-            D((3, 3)), D((3, 3)),
+            D((9,)), D((2, K, HALVES)), D((2, K, HALVES)),
+            D((4, 3)), D((4, 3)),
             D((K,)), D,
             D((3,)), D((3, NX * NC)), D((3,)), D((3, NX * NC)), D((3,)),
             D((2,)), D((2,)), D, D,

time: 100 us -> 94.9 us (0.949)
  the two profiles are of different devices: /device:TPU:17 before, /device:TPU:31 now
where the time goes in v4:
time: 94.9 us; the launch traced here: 94.7 us
  Pallas kernels  91.3 us (96%)
  local copies, waits for them, and re-layouts  2.73 us (3%)
    pallas_call x1, Pallas kernels, body(): pl.pallas_call(functools.partial(kernel, dims), out_shape=jax.ShapeDtypeS...  91.3 us

profile of v4, /device:TPU:31, one launch (start us, length us, event | category | flops | bytes accessed | tf_op | source)
XLA Modules:
  0.0 94.7 jit_solution(17650105591357506959)
XLA Ops:
  0.6 91.3 %shard_map.103 = f32[160,128]{1,0:T(8,128)} custom-call(bf16[128,4096]{1,0:T(8,128)(2,1)} %teacher.1, s32[1,128]{1,0:T(1,128)} %bitcast.9, bf16[128,2048]{1,0:T(8,128)(2,1)} %student.1, bf16[128,2048]{1,0:T(8,128)(2,1)} %projected.1, bf16[128,2048]{1,0:T(8,128)(2,1)} %mlp.1, bf16[8192,128]{1,0:T(8,128)(2,1)} %gate.1, bf16[8192,128]{1,0:T(8,128)(2,1)} %up.1, ...), custom_call_target="tpu_custom_call" | custom-call | tf_op jit(solution)/shard_map/pallas_call | solution.py:551
  92.0 1.4 %slice_bitcast_fusion = (f32[128,64]{0,1:T(8,128)}, f32[128,64]{0,1:T(8,128)}) fusion(f32[160,128]{1,0:T(8,128)} %shard_map.103), kind=kLoop, calls=%fused_computation | loop fusion | bytes 131072 | tf_op jit(solution)/shard_map/transpose | solution.py:561
  93.4 1.3 %slice_bitcast_fusion.2 = f32[128,1,32]{0,2,1:T(8,128)} fusion(f32[160,128]{1,0:T(8,128)} %shard_map.103), kind=kLoop, calls=%fused_computation.2 | loop fusion | bytes 32768 | tf_op jit(solution)/shard_map/broadcast_in_dim | solution.py:561

commit v5 on v4

--- a/solution.py
+++ b/solution.py
@@ -477,12 +477,14 @@
     for q in range(NZ):
         arrived(RB3.at[q], rb_r.at[q])
         result = RB3[q].astype(F32) if result is None else result + RB3[q].astype(F32)
-    out[0 : 2 * R, :] = result
+    flipped = jnp.transpose(result)
+    out[:, 0:R] = flipped[:, 0:R]
+    out[:, R : 2 * R] = flipped[:, R : 2 * R]
     result = None
     for q in range(NZ):
         arrived(RBP.at[q], rp_r.at[q])
         result = RBP[q].astype(F32) if result is None else result + RBP[q].astype(F32)
-    out[2 * R : 2 * R + RP, :] = result
+    out[:, 2 * R : 2 * R + RP] = jnp.transpose(result)
 
     def left(own, ref, sem):
         @pl.when(jnp.logical_not(own))
@@ -550,7 +552,7 @@
         ]
         res = pl.pallas_call(
             functools.partial(kernel, dims),
-            out_shape=jax.ShapeDtypeStruct((2 * R + RP, H), F32),
+            out_shape=jax.ShapeDtypeStruct((H, 2 * R + RP), F32),
             in_specs=[pl.BlockSpec(memory_space=pl.ANY)] * 8,
             out_specs=pl.BlockSpec(memory_space=pltpu.VMEM),
             scratch_shapes=scratch,
@@ -558,7 +560,7 @@
                 collective_id=0, has_side_effects=True, vmem_limit_bytes=VMEM_LIMIT
             ),
         )(teacher_rows, row_map.reshape(1, TOK), student_hidden, projected, mlp_input, gate_bucket, up_bucket, down_bucket)
-        return res[2 * R :].T[:, None, :], res[:R].T, res[R : 2 * R].T
+        return res[:, None, 2 * R :], res[:, :R], res[:, R : 2 * R]
 
     in_specs = (
         P("dp", "tensor"), P("dp"), P("dp", "tensor"), P("dp", "tensor"), P("dp", "tensor"),

time: 94.9 us -> 96.3 us (1.015)
  local copies, waits for them, and re-layouts: 2.73 us -> 3.92 us
    unnamed x0 -> x3, local copies, waits for them, and re-layouts: none -> 2.08 us
    transpose x1 -> x0, local copies, waits for them, and re-layouts: 1.4 us -> none  [body(): return (res[2 * R:].T[:, None, :], res[:R].T, res[R:2 * R].T)]
    slice x0 -> x1, local copies, waits for them, and re-layouts: none -> 0.99 us  [body(): return (res[:, None, 2 * R:], res[:, :R], res[:, R:2 * R])]
where the time goes in v5:
time: 96.3 us; the launch traced here: 96.1 us
  Pallas kernels  91.5 us (95%)
  local copies, waits for them, and re-layouts  3.92 us (4%)
    pallas_call x1, Pallas kernels, body(): pl.pallas_call(functools.partial(kernel, dims), out_shape=jax.ShapeDtypeS...  91.5 us
    unnamed x3, local copies, waits for them, and re-layouts  2.08 us

profile of v5, /device:TPU:31, one launch (start us, length us, event | category | flops | bytes accessed | tf_op | source)
XLA Modules:
  0.0 96.1 jit_solution(16092691577618990575)
XLA Ops:
  0.6 91.5 %shard_map.103 = f32[128,160]{1,0:T(8,128)} custom-call(bf16[128,4096]{1,0:T(8,128)(2,1)} %teacher.1, s32[1,128]{1,0:T(1,128)} %bitcast.3, bf16[128,2048]{1,0:T(8,128)(2,1)} %student.1, bf16[128,2048]{1,0:T(8,128)(2,1)} %projected.1, bf16[128,2048]{1,0:T(8,128)(2,1)} %mlp.1, bf16[8192,128]{1,0:T(8,128)(2,1)} %gate.1, bf16[8192,128]{1,0:T(8,128)(2,1)} %up.1, ...), custom_call_target="tpu_custom_call" | custom-call | tf_op jit(solution)/shard_map/pallas_call | solution.py:553
  92.2 0.8 slice_bitcast_fusion
  93.0 0.7 copy.11
  93.7 1.0 %fusion = (f32[128,64]{1,0:T(8,128)S(1)}, f32[128,64]{1,0:T(8,128)S(1)}) fusion(f32[128,160]{1,0:T(8,128)} %shard_map.103), kind=kLoop, calls=%fused_computation.1 | loop fusion | bytes 131072 | tf_op jit(solution)/shard_map/slice | solution.py:563
  94.7 0.7 copy.13
  95.4 0.7 copy.12
